TPU v7x, 512 devices: a whole 4x8x8 slice. The times are simulated.
512 devices in a mesh: box: 128 (over y, z, core), rep: 4 (over x).
Axes of the slice: x: 4, y: 8, z: 8, core: 2. Of those that a mesh axis runs over, the one named last changes fastest.
Arguments:
- multipoles: float32 [121, 32768], P(None, 'box'), may hold values from -6 to 6
- parent_locals: float32 [121, 8192], P(None, ('box', 'rep')), may hold values from -6 to 6
- box_counts: int32 [128], P('box'), may hold values from 128 to 256, as said below
- box_ids: int32 [32768], P('box'), may hold values from 0 to 65534, as said below
- pair_source: int32 [128, 32768], P('rep', 'box'), may hold values from 0 to 1280, as said below
- export_slots: int32 [16384, 32], P('box', 'rep'), may hold values from 0 to 256, as said below
- operators: float32 [128, 14641], P('rep'), may hold values from -0.03125 to 0.03125
- shifters: float32 [8, 14641], replicated, may hold values from -0.5 to 0.5
Outputs:
- local_fields: float32 [121, 32768], P(None, ('box', 'rep'))
Inputs may be any that keep to these rules, and one draw needn't show every extreme that they name: `box_counts`: index b of box holds live boxes in its slots 0 to count - 1. `box_ids`: rising within each index of box; index b's ids lie in [2 * 256 b, 2 * 256 (b + 1)), its first a multiple of 8, and the parents (id // 8) of its slots lie within 64 consecutive level-5 ids starting at its first slot's parent. `pair_source`: values below 256 are the device's own slots, other than the target; values from 256 to 256 + 128 * 8 - 1 are entries received from peer e at position j (value 256 + e * 8 + j) and name only filled export positions; the value 256 + 128 * 8 means no partner, and every slot at or beyond the device's count holds it. `export_slots`: filled positions of a row come first and name live slots of the sender; 256 marks an empty position; every row has at least one filled position.
All inputs are finite; a program needn't handle non-finite values.
Results may differ from a plain program's by a relative error of at most 0.0001.
Values sent between devices are 32-bit elements; how exact they have to be, the bound alone decides.
No kernel may reach another device: no remote copies, remote signals or barrier semaphores. Data moves between devices by JAX's collectives and lax.ppermute only.
A program may use at most 64 MiB of HBM per device.

v0:
```python
import jax
import jax.numpy as jnp
from jax import lax
from jax.sharding import PartitionSpec as P

ORDER = 10


def degree_parity(length):
    position = jnp.arange(length, dtype=jnp.int32)
    degree = jnp.zeros((length,), jnp.int32)
    for level in range(1, ORDER + 1):
        degree = degree + (position >= level * level).astype(jnp.int32)
    return (1 - 2 * (degree % 2)).astype(jnp.float32)


def shift_children(fathers, shift_all, child_ids, first_id, coeffs):
    highest = lax.Precision.HIGHEST
    father_slot = child_ids // 8 - first_id // 8
    father_rows = jnp.arange(fathers.shape[1], dtype=jnp.int32)
    chooser = (father_rows[:, None] == father_slot[None, :]).astype(jnp.float32)
    picked = jnp.dot(fathers, chooser, precision=highest, preferred_element_type=jnp.float32)
    corners = jnp.arange(8, dtype=jnp.int32)
    onehot = (child_ids[None, :] % 8 == corners[:, None]).astype(jnp.float32)
    stacked = (onehot[:, None, :] * picked[None, :, :]).reshape(8 * coeffs, child_ids.shape[0])
    return jnp.dot(shift_all, stacked, precision=highest, preferred_element_type=jnp.float32)


def on_device(
    multipoles, parent_locals, box_counts, box_ids, pair_source, export_slots, operators, shifters
):
    highest = lax.Precision.HIGHEST
    coeffs, slots = multipoles.shape
    quarters = lax.axis_size("rep")
    cls_dev = operators.shape[0]
    width = (coeffs + 127) // 128 * 128
    export_flat = export_slots.reshape(-1)
    slot_range = jnp.arange(slots, dtype=jnp.int32)
    selector = (slot_range[:, None] == export_flat[None, :]).astype(jnp.float32)
    outgoing = jnp.dot(multipoles, selector, precision=highest, preferred_element_type=jnp.float32)
    arrived = lax.all_to_all(outgoing, "box", split_axis=1, concat_axis=1, tiled=True)
    sent_count = arrived.shape[1]
    row_table = jnp.concatenate(
        [multipoles.T, arrived.T, jnp.zeros((1, coeffs), jnp.float32)], axis=0
    )
    row_table = jnp.pad(row_table, ((0, 0), (0, width - coeffs)))
    columns = row_table.shape[0]
    parity = degree_parity(coeffs)
    parity_wide = jnp.pad(parity, (0, width - coeffs))
    signed_rows = row_table[:slots] * parity_wide[None, :]
    translate = jnp.pad(
        operators.reshape(cls_dev, coeffs, coeffs),
        ((0, 0), (0, width - coeffs), (0, width - coeffs)),
    )
    class_step = 8
    nearby = jnp.zeros((slots, width), jnp.float32)
    reverse = jnp.zeros((columns, width), jnp.float32)
    for start_class in range(0, cls_dev, class_step):
        part_mats = translate[start_class : start_class + class_step]
        partner = pair_source[start_class : start_class + class_step]
        picked = jnp.take(row_table, partner, axis=0)
        nearby = nearby + jnp.einsum(
            "cjk,csk->sj", part_mats, picked, precision=highest, preferred_element_type=jnp.float32
        )
        mirrored = (
            jnp.einsum(
                "cjk,sk->csj",
                part_mats,
                signed_rows,
                precision=highest,
                preferred_element_type=jnp.float32,
            )
            * parity_wide[None, None, :]
        )
        reverse = reverse + jax.ops.segment_sum(
            mirrored.reshape(-1, width), partner.reshape(-1), num_segments=columns
        )
    outbound = reverse[slots : slots + sent_count, :coeffs].T
    returned = lax.all_to_all(outbound, "box", split_axis=1, concat_axis=1, tiled=True)
    landed = jnp.dot(returned, selector.T, precision=highest, preferred_element_type=jnp.float32)
    accumulated = (nearby + reverse[:slots])[:, :coeffs].T + landed
    fathers = lax.all_gather(parent_locals, "rep", axis=1, tiled=True)
    shift_all = shifters.reshape(8, coeffs, coeffs).transpose(1, 0, 2).reshape(coeffs, 8 * coeffs)
    rep_index = lax.axis_index("rep")
    quarter = slots // quarters
    offset = rep_index * quarter
    weight = (rep_index == 0).astype(jnp.float32)
    accumulated = accumulated + weight * shift_children(
        fathers, shift_all, box_ids, box_ids[0], coeffs
    )
    summed = lax.psum(accumulated, "rep")
    portion = lax.dynamic_slice_in_dim(summed, offset, quarter, 1)
    occupied = offset + jnp.arange(quarter, dtype=jnp.int32) < box_counts[0]
    return jnp.where(occupied[None, :], portion, 0.0)


def solution(mesh):
    return jax.shard_map(
        on_device,
        mesh=mesh,
        in_specs=(
            P(None, "box"),
            P(None, ("box", "rep")),
            P("box"),
            P("box"),
            P("rep", "box"),
            P("box", "rep"),
            P("rep", None),
            P(),
        ),
        out_specs=P(None, ("box", "rep")),
        check_vma=False,
    )
```

profile of v0, /device:TPU:40, one launch (start us, length us, event | category | flops | bytes accessed | tf_op | source)
XLA Modules:
  0.0 242.1 jit_solution(1058664579881265123)
XLA Ops:
  6.5 0.8 copy.11
  7.3 0.1 eq.53
  7.4 2.4 %convolution_bitcast_fusion = f32[121,128,8]{0,2,1:T(8,128)} fusion(f32[121,256]{1,0:T(8,128)} %param.10, s32[1024]{0:T(1024)S(1)} %eq.53), kind=kOutput, calls=%fused_computation.16 | convolution fusion | flops 381157376 | bytes 623616 | tf_op jit(solution)/shard_map/dot_general | solution.py:40
  9.9 17.3 %all-to-all-start = ((f32[121,128,8]{0,2,1:T(8,128)}), f32[121,128,8]{0,2,1:T(8,128)S(1)}, u32[]{:S(2)}, u32[]{:S(2)}) async-start(f32[121,128,8]{0,2,1:T(8,128)} %convolution_bitcast_fusion), calls=%async_computation | async-start | bytes 1048576 | tf_op jit(solution)/shard_map/all_to_all | solution.py:41
  27.2 1.2 slice.51
  29.7 1.0 copy.10
  30.7 0.0 copy-done.5
  30.7 0.6 compare_and_fusion.3
  32.7 0.0 copy-done.14
  32.7 0.6 and_select_fusion.1
  33.3 4.8 %reshape.63 = f32[32,121,121]{2,1,0:T(8,128)S(1)} reshape(f32[32,14641]{1,0:T(8,128)} %param.16) | data formatting | bytes 3748096 | tf_op jit(solution)/shard_map/reshape | solution.py:52
  38.1 0.6 copy.16
  38.7 0.6 copy.17
  39.3 0.6 copy.18
  39.9 0.6 copy.19
  40.5 0.6 broadcast_clamp_fusion
  41.2 0.6 pad.17.clone
  41.8 0.0 copy-done.9
  41.8 12.4 %all_gather.3 = f32[121,64]{0,1:T(8,128)S(1)} all-gather(f32[121,16]{0,1:T(8,128)S(1)} %copy-done.9), channel_id=1, replica_groups=mesh['box'=128,'rep'=4] {'rep'}, dimensions={1}, use_global_device_ids=true | all-gather | bytes 38720 | tf_op jit(solution)/shard_map/all_gather | solution.py:82
  54.2 0.6 broadcast_clamp_fusion.1
  54.8 0.6 broadcast_clamp_fusion.2
  55.4 0.6 broadcast_clamp_fusion.3
  56.0 0.3 convolution_bitcast_fusion.2
  56.3 0.0 all-to-all-done
  56.3 0.9 maximum_maximum_fusion
  57.2 2.0 convolution_multiply_fusion.3
  59.2 2.0 convolution_multiply_fusion.2
  61.2 2.0 convolution_multiply_fusion.1
  63.1 2.0 convolution_multiply_fusion
  65.1 13.1 %scatter_custom_fusion = f32[1281,128]{1,0:T(8,128)} fusion(s32[2048]{0:T(1024)} %bitcast.112, f32[2048,128]{1,0:T(8,128)} %bitcast.103, f32[]{:T(128)} %constant.76.clone.1), kind=kCustom, calls=%fused_computation.54 | custom fusion | flops 262144 | bytes 656384 | tf_op jit(solution)/shard_map/scatter-add | solution.py:75
  78.2 13.1 %scatter_custom_fusion.1 = f32[1281,128]{1,0:T(8,128)} fusion(s32[2048]{0:T(1024)} %bitcast.111, f32[2048,128]{1,0:T(8,128)} %bitcast.102, f32[]{:T(128)} %constant.76.clone.1), kind=kCustom, calls=%fused_computation.52 | custom fusion | flops 262144 | bytes 656384 | tf_op jit(solution)/shard_map/scatter-add | solution.py:75
  91.3 1.4 add.118
  92.7 13.1 %scatter_custom_fusion.3 = f32[1281,128]{1,0:T(8,128)} fusion(s32[2048]{0:T(1024)} %bitcast.110, f32[2048,128]{1,0:T(8,128)} %bitcast.101, f32[]{:T(128)} %constant.76.clone.1), kind=kCustom, calls=%fused_computation.50 | custom fusion | flops 262144 | bytes 656384 | tf_op jit(solution)/shard_map/scatter-add | solution.py:75
  105.8 12.4 %scatter_fusion = f32[1281,128]{1,0:T(8,128)S(1)} fusion(f32[1281,128]{1,0:T(8,128)S(1)} %add.118, s32[2048]{0:T(1024)} %bitcast.105, f32[2048,128]{1,0:T(8,128)} %bitcast.95), kind=kCustom, calls=%fused_computation.6 | custom fusion | flops 262144 | bytes 3153920 | tf_op jit(solution)/shard_map/scatter-add | solution.py:75
  118.2 1.2 add.119
  119.4 0.0 copy-start.3
  119.4 0.8 copy-done.3
  120.2 0.8 slice_bitcast_fusion
  121.1 17.7 %all-to-all-start.1 = ((f32[121,128,8]{0,2,1:T(8,128)}), f32[121,128,8]{0,2,1:T(8,128)}, u32[]{:S(2)}, u32[]{:S(2)}) async-start(f32[121,128,8]{0,2,1:T(8,128)} %slice_bitcast_fusion), calls=%async_computation.1 | async-start | bytes 1048576 | tf_op jit(solution)/shard_map/all_to_all | solution.py:79
  138.8 0.0 all-reduce.5.cloned.1.call-start
  138.8 0.0 copy-done.13
  138.9 1.8 reshape.68
  140.6 1.7 fusion.2
  142.4 0.0 copy-start.6
  142.4 8.4 %gather_fusion.3 = f32[2048,128]{1,0:T(8,128)} fusion(f32[1281,128]{1,0:T(8,128)S(1)} %pad.12, s32[2048]{0:T(1024)} %broadcast_clamp_fusion), kind=kCustom, calls=%fused_computation.3.clone | custom fusion | bytes 2105344 | tf_op jit(solution)/shard_map/jit(_take)/gather | solution.py:61
  150.8 7.6 %gather_fusion.2 = f32[2048,128]{1,0:T(8,128)} fusion(f32[1281,128]{1,0:T(8,128)S(1)} %pad.12, s32[2048]{0:T(1024)S(1)} %copy-done.6), kind=kCustom, calls=%fused_computation.2.clone | custom fusion | bytes 2105344 | tf_op jit(solution)/shard_map/jit(_take)/gather | solution.py:61
  158.4 0.0 copy-done.7
  158.4 7.6 %gather_fusion.1 = f32[2048,128]{1,0:T(8,128)} fusion(f32[1281,128]{1,0:T(8,128)S(1)} %pad.12, s32[2048]{0:T(1024)S(1)} %copy-done.7), kind=kCustom, calls=%fused_computation.1.clone | custom fusion | bytes 2105344 | tf_op jit(solution)/shard_map/jit(_take)/gather | solution.py:61
  166.0 7.6 %gather_fusion = f32[2048,128]{1,0:T(8,128)} fusion(f32[1281,128]{1,0:T(8,128)S(1)} %pad.12, s32[2048]{0:T(1024)S(1)} %copy-done.8), kind=kCustom, calls=%fused_computation.clone | custom fusion | bytes 2105344 | tf_op jit(solution)/shard_map/jit(_take)/gather | solution.py:61
  173.6 2.4 convolution_bitcast_fusion.3
  176.0 1.1 convolution_bitcast_fusion.4
  177.1 0.1 copy-done.1
  177.2 0.0 copy-done.10
  177.2 1.1 convolution_bitcast_fusion.5
  178.3 0.0 slice-start
  178.3 0.0 copy-done
  178.3 1.1 convolution_bitcast_fusion.6
  179.4 0.0 all-to-all-done.1
  179.4 0.0 slice-done
  179.4 0.0 copy-done.4
  179.4 2.4 fusion
  181.8 0.0 all-reduce.5.cloned.1.call-update
  182.5 51.3 %all-reduce.5.cloned.1.call-done = f32[121,256]{0,1:T(8,128)} async-done(((f32[121,256]{0,1:T(8,128)}), f32[121,256]{0,1:T(8,128)}) %all-reduce.5.cloned.1.call-update) | async-done | bytes 123920 | tf_op jit(solution)/shard_map/psum | solution.py:91
  233.8 1.4 dynamic-slice_select_fusion
  (28 shorter events, 0.1 us)
Async XLA Ops:
  6.5 26.1 %copy-start.14 = (s32[256]{0:T(256)S(1)}, s32[256]{0:T(256)}, u32[]{:S(2)}) copy-start(s32[256]{0:T(256)} %param.13) | copy-start | bytes 3076
  6.5 24.2 %copy-start.5 = (s32[32,256]{1,0:T(8,128)S(1)}, s32[32,256]{1,0:T(8,128)}, u32[]{:S(2)}) copy-start(s32[32,256]{1,0:T(8,128)} %param.14) | copy-start | bytes 98308
  9.9 46.4 %all-to-all-start = ((f32[121,128,8]{0,2,1:T(8,128)}), f32[121,128,8]{0,2,1:T(8,128)S(1)}, u32[]{:S(2)}, u32[]{:S(2)}) async-start(f32[121,128,8]{0,2,1:T(8,128)} %convolution_bitcast_fusion), calls=%async_computation | async-start | bytes 1048576 | tf_op jit(solution)/shard_map/all_to_all | solution.py:41
  31.3 10.4 %copy-start.9 = (f32[121,16]{0,1:T(8,128)S(1)}, f32[121,16]{0,1:T(8,128)}, u32[]{:S(2)}) copy-start(f32[121,16]{0,1:T(8,128)} %param.11) | copy-start | bytes 23236
  119.4 0.8 copy-start.3
  120.2 18.6 %copy-start.13 = (s32[256]{0:T(256)S(1)}, s32[256]{0:T(256)}, u32[]{:S(2)}) copy-start(s32[256]{0:T(256)} %get-tuple-element.18) | copy-start | bytes 3076
  121.1 58.3 %all-to-all-start.1 = ((f32[121,128,8]{0,2,1:T(8,128)}), f32[121,128,8]{0,2,1:T(8,128)}, u32[]{:S(2)}, u32[]{:S(2)}) async-start(f32[121,128,8]{0,2,1:T(8,128)} %slice_bitcast_fusion), calls=%async_computation.1 | async-start | bytes 1048576 | tf_op jit(solution)/shard_map/all_to_all | solution.py:79
  138.8 95.0 %all-reduce.5.cloned.1.call-start = ((), (), s32[]{:S(2)}) async-start(), calls=%async_computation.2 | async-start | bytes 262144 | tf_op jit(solution)/shard_map/psum | solution.py:91
  142.4 8.4 %copy-start.6 = (s32[2048]{0:T(1024)S(1)}, s32[2048]{0:T(1024)}, u32[]{:S(2)}) copy-start(s32[2048]{0:T(1024)} %broadcast_clamp_fusion.1) | copy-start | bytes 24580
  150.8 7.6 %copy-start.7 = (s32[2048]{0:T(1024)S(1)}, s32[2048]{0:T(1024)}, u32[]{:S(2)}) copy-start(s32[2048]{0:T(1024)} %broadcast_clamp_fusion.2) | copy-start | bytes 24580
  158.4 7.6 %copy-start.8 = (s32[2048]{0:T(1024)S(1)}, s32[2048]{0:T(1024)}, u32[]{:S(2)}) copy-start(s32[2048]{0:T(1024)} %broadcast_clamp_fusion.3) | copy-start | bytes 24580
  166.0 7.6 %copy-start.12 = (pred[8,256]{1,0:T(8,128)(4,1)S(1)}, pred[8,256]{1,0:T(8,128)(4,1)}, u32[]{:S(2)}) copy-start(pred[8,256]{1,0:T(8,128)(4,1)} %get-tuple-element.7) | copy-start | bytes 6148
  173.6 2.4 copy-start.2
  173.6 2.4 copy-start.11
  176.0 1.2 copy-start.1
  176.0 1.2 copy-start.10
  177.1 1.3 copy-start
  178.3 1.1 slice-start
  178.3 1.1 copy-start.4
Sparse Core Ops, SparseCore 0:
  181.9 51.8 all-reduce.4
where the time goes:
time: 244 us; the launch traced here: 242 us
  other arithmetic  60.2 us (25%)
  waiting for transfers between devices  51.3 us (21%)
  local copies, waits for them, and re-layouts  45.8 us (19%)
  starting transfers between devices  35.1 us (14%)
  matrix products  20.3 us (8%)
  between operations  17 us (7%)
  blocking collectives  12.4 us (5%)
    scatter-add x4, other arithmetic, on_device(): jax.ops.segment_sum(mirrored.reshape(-1, width), partner.reshape(-1), num...  51.7 us
    psum x1, waiting for transfers between devices, on_device(): summed = lax.psum(accumulated, 'rep')  51.3 us
    gather x4, local copies, waits for them, and re-layouts, on_device(): picked = jnp.take(row_table, partner, axis=0)  31.1 us
    all_to_all x1, starting transfers between devices, on_device(): lax.all_to_all(outbound, 'box', split_axis=1, concat_axis=1, tiled=True)  17.7 us
    all_to_all x1, starting transfers between devices, on_device(): lax.all_to_all(outgoing, 'box', split_axis=1, concat_axis=1, tiled=True)  17.3 us
    all_gather x1, blocking collectives, on_device(): fathers = lax.all_gather(parent_locals, 'rep', axis=1, tiled=True)  12.4 us
    dot_general x4, matrix products, on_device(): jnp.einsum('cjk,sk->csj', part_mats, signed_rows, precision=highest, pref...  7.92 us
    dot_general x4, matrix products, on_device(): jnp.einsum('cjk,csk->sj', part_mats, picked, precision=highest, preferred...  5.54 us
  transfers between devices with their start and end apart: 3, of which 1 were waited for; matrix products, arithmetic and copies ran while one was open for 22% of the time, Pallas kernels for 0%

commit v1 on v0

v1 whole, which is shorter than its diff:
```python
import jax
import jax.numpy as jnp
from jax import lax
from jax.experimental import pallas as pl
from jax.experimental.pallas import tpu as pltpu
from jax.sharding import PartitionSpec as P

ORDER = 10
SEND = 8
Z_BITS = 3
Z_CHIPS = 1 << Z_BITS
LANES = 128
BF = jnp.bfloat16
F32 = jnp.float32
VMEM_LIMIT = 24 * 1024 * 1024


def mm(a, b):
    return jnp.dot(a, b, preferred_element_type=F32)


def split_hl(x):
    hi = x.astype(BF)
    lo = (x - hi.astype(F32)).astype(BF)
    return jnp.concatenate([hi, lo], axis=1)


def fold(x):
    half = x.shape[1] // 2
    return x[:, :half] + x[:, half:]


def parity_lanes(rows):
    k = lax.broadcasted_iota(jnp.int32, (rows, LANES), 1)
    degree = jnp.zeros((rows, LANES), jnp.int32)
    for level in range(1, ORDER + 1):
        degree = degree + jnp.where(k >= level * level, 1, 0)
    return jnp.where((degree & 1) == 0, 1.0, -1.0).astype(F32)


def onehot(mask):
    return jnp.where(mask, 1.0, 0.0).astype(BF)


def matrices_to_rows(src, first, coeffs, out):
    total = coeffs * coeffs
    lane = lax.broadcasted_iota(jnp.int32, (8, LANES), 1)
    for j in range(coeffs):
        base = j * coeffs // LANES * LANES
        shift = j * coeffs - base
        stop = min(base + 2 * LANES, total)
        wide = src[pl.ds(first, 8), base:stop]
        if stop < base + 2 * LANES:
            wide = jnp.concatenate([wide, jnp.zeros((8, base + 2 * LANES - stop), F32)], axis=1)
        if shift:
            wide = pltpu.roll(wide, 2 * LANES - shift, 1)
        row = jnp.where(lane < coeffs, wide[:, :LANES], 0.0)
        out[pl.ds(first * LANES + j, 8, stride=LANES), :] = row
    for j in range(coeffs, LANES):
        out[pl.ds(first * LANES + j, 8, stride=LANES), :] = jnp.zeros((8, LANES), F32)


def chip_ranks(chips):
    rows = chips // Z_CHIPS
    return [((r // Z_CHIPS + r) % Z_CHIPS % rows) * Z_CHIPS + r % Z_CHIPS for r in range(chips)]


def rank_columns(ex, core):
    nb = ex.shape[1]
    rows = nb // 2 // Z_CHIPS
    source = lax.broadcasted_iota(jnp.int32, (nb, nb), 0)
    place = lax.broadcasted_iota(jnp.int32, (nb, nb), 1)
    rank = place >> 1
    z = rank & (Z_CHIPS - 1)
    y = (lax.shift_right_logical(rank, Z_BITS) + z) & (rows - 1)
    column = ((y * Z_CHIPS + z) << 1) | ((place & 1) ^ core)
    wide = jnp.concatenate([ex, ex], axis=0).astype(F32).astype(BF)
    return mm(wide, onehot(source == column))[: ex.shape[0]].astype(jnp.int32)


def far_order(ps, slots, nb, core):
    rows = nb // 2 // Z_CHIPS
    entry = ps - slots
    peer = entry >> 3
    z = (peer >> 1) & (Z_CHIPS - 1)
    y = peer >> (1 + Z_BITS)
    rank = ((y - z) & (rows - 1)) * Z_CHIPS + z
    moved = (((rank << 1) | ((peer & 1) ^ core)) << 3) | (entry & (SEND - 1))
    return jnp.where((entry >= 0) & (entry < nb * SEND), slots + moved, ps)


def spread_rows(row, rows):
    tile = jnp.broadcast_to(row, (16, row.shape[1])).astype(F32).astype(BF)
    return jnp.concatenate([tile] * (rows // 16), axis=0)


def pick16(mask):
    return jnp.where(mask, jnp.ones((), BF), jnp.zeros((), BF))


def export_kernel(
    core_ref, mult_in, ex_in, keep_ref, give_ref, mrow_ref, mult_ref, ex_ref, all_ref, mult_sem, ex_sem
):
    fetch_mult = pltpu.make_async_copy(mult_in, mult_ref, mult_sem)
    fetch_ex = pltpu.make_async_copy(ex_in, ex_ref, ex_sem)
    fetch_mult.start()
    fetch_ex.start()
    fetch_ex.wait()
    coeffs, slots = mult_ref.shape
    nb = ex_ref.shape[1]
    ex = rank_columns(ex_ref[...], core_ref[0])
    ex = jnp.concatenate([ex, jnp.zeros((LANES - SEND, nb), jnp.int32)], axis=0).T
    fetch_mult.wait()
    wide = jnp.concatenate([mult_ref[...], jnp.zeros((LANES - coeffs, slots), F32)], axis=0)
    rows = wide.T
    mrow_ref[...] = rows
    table = split_hl(rows)
    lane = lax.broadcasted_iota(jnp.int32, (nb, slots), 1)
    for j in range(SEND):
        picked = mm(onehot(lane == ex[:, j : j + 1]), table)
        all_ref[pl.ds(j, nb, stride=SEND), :] = fold(picked)
    pairs = all_ref[...].reshape(nb // 2, 2 * SEND, LANES)
    keep_ref[...] = pairs[:, :SEND, :]
    give_ref[...] = pairs[:, SEND:, :]


def reverse_kernel(
    core_ref,
    op_in,
    mrow_ref,
    ps_ref,
    w_out,
    own_ref,
    keep_ref,
    give_ref,
    op_ref,
    t_ref,
    w_ref,
    acc_ref,
    op_sem,
    w_sem,
):
    classes = op_ref.shape[0]
    coeffs = 121
    slots = mrow_ref.shape[0]
    columns = acc_ref.shape[0]
    group = 8
    block = 256

    def fetch(k):
        rows = pl.ds(pl.multiple_of(k * 8, 8), 8)
        return pltpu.make_async_copy(op_in.at[rows, :], op_ref.at[rows, :], op_sem.at[k])

    for k in range(classes // 8):
        fetch(k).start()

    @pl.loop(0, classes // 8)
    def _(k):
        fetch(k).wait()
        matrices_to_rows(op_ref, pl.multiple_of(k * 8, 8), coeffs, t_ref)

    sign = parity_lanes(slots)
    moments = split_hl(mrow_ref[...] * sign)
    acc_ref[...] = jnp.zeros_like(acc_ref)
    row_id = lax.broadcasted_iota(jnp.int32, (block, slots), 0).astype(F32).astype(BF)

    @pl.loop(0, classes // group)
    def _(g):
        mirrors = []
        for i in range(group):
            c = g * group + i
            w = split_hl(t_ref[pl.ds(pl.multiple_of(c * LANES, LANES), LANES), :].T)
            w_ref[c] = w
            mirrors.append(split_hl(fold(mm(moments, jnp.concatenate([w, w], axis=0)))))
        m = jnp.concatenate(mirrors, axis=0)
        ps = ps_ref[pl.ds(pl.multiple_of(g * group, group), group), :]
        ps = far_order(ps, slots, (columns - slots) // SEND, core_ref[0])
        for start in range(0, columns, block):
            here = ps - start
            hot = jnp.concatenate(
                [pick16(row_id == spread_rows(here[i : i + 1, :], block)) for i in range(group)],
                axis=1,
            )
            acc_ref[start : start + block, :] += mm(hot, m)

    copy = pltpu.make_async_copy(w_ref, w_out, w_sem)
    copy.start()
    own_ref[...] = fold(acc_ref[:slots, :]) * sign
    far = columns - slots
    sums = fold(acc_ref[slots:, :]) * parity_lanes(far)
    pairs = sums.reshape(far // (2 * SEND), 2 * SEND, LANES)
    keep_ref[...] = pairs[:, :SEND, :]
    give_ref[...] = pairs[:, SEND:, :]
    copy.wait()


def forward_kernel(
    rep_ref,
    core_ref,
    w_in,
    mrow_ref,
    arr_ref,
    ps_ref,
    ids_ref,
    par_ref,
    sh_ref,
    own_ref,
    out_ref,
    w_ref,
    table_ref,
    cols_ref,
    u_ref,
    acc_ref,
    w_sem,
):
    copy = pltpu.make_async_copy(w_in, w_ref, w_sem)
    copy.start()
    classes = w_ref.shape[0]
    slots = mrow_ref.shape[0]
    columns = table_ref.shape[0]
    coeffs = 121
    block = 256
    table_ref[:slots, :] = split_hl(mrow_ref[...])
    table_ref[slots:, :] = split_hl(arr_ref[...])
    ps = far_order(ps_ref[...], slots, (columns - slots) // SEND, core_ref[0])
    pst = jnp.concatenate([ps, jnp.zeros((LANES - classes, slots), jnp.int32)], axis=0).T
    for c in range(classes):
        cols_ref[c] = jnp.broadcast_to(pst[:, c : c + 1], (slots, LANES))

    acc_ref[...] = jnp.zeros_like(acc_ref)
    lane = lax.broadcasted_iota(jnp.int32, (slots, block), 1).astype(F32).astype(BF)
    group = 4
    copy.wait()

    @pl.loop(0, classes // group)
    def _(g):
        hots = []
        for i in range(group):
            col = cols_ref[g * group + i]
            parts = []
            for start in range(0, columns, block):
                here = (col - start).astype(F32).astype(BF)
                parts.append(pick16(lane == jnp.concatenate([here] * (block // LANES), axis=1)))
            hots.append(jnp.concatenate(parts, axis=1))
        picked = mm(jnp.concatenate(hots, axis=0), table_ref[...]).astype(BF)
        total = None
        for i in range(group):
            w = w_ref[g * group + i]
            part = mm(picked[i * slots : (i + 1) * slots], jnp.concatenate([w, w], axis=0))
            total = part if total is None else total + part
        acc_ref[...] += total

    matrices_to_rows(sh_ref, 0, coeffs, u_ref)
    parents = par_ref[...]
    held = parents.shape[0]
    parents = jnp.concatenate([parents, jnp.zeros((held, LANES - coeffs), F32)], axis=1)
    lhs = split_hl(parents)
    moved = []
    for o in range(8):
        w = split_hl(u_ref[o * LANES : (o + 1) * LANES, :].T)
        moved.append(fold(mm(lhs, jnp.concatenate([w, w], axis=0))))
    moved = split_hl(jnp.concatenate(moved, axis=0))
    ids = jnp.broadcast_to(ids_ref[...], (8, slots))
    parent = lax.shift_right_logical(ids, 3)
    q = parent - parent[:, 0:1] - rep_ref[0] * held
    code = jnp.where((q >= 0) & (q < held), (ids & 7) * held + q, -1)
    code = jnp.concatenate([code, jnp.zeros((LANES - 8, slots), jnp.int32)], axis=0).T
    pick = lax.broadcasted_iota(jnp.int32, (slots, 8 * held), 1)
    shifted = fold(mm(onehot(pick == code[:, 0:1]), moved))
    out_ref[...] = fold(acc_ref[...]) + own_ref[...] + shifted


def landing_kernel(core_ref, cnt_ref, ex_ref, ret_ref, part_ref, out_ref):
    slots = part_ref.shape[0]
    nb = ex_ref.shape[1]
    row = lax.broadcasted_iota(jnp.int32, (slots, nb), 0)
    ex = rank_columns(ex_ref[...], core_ref[0])
    hots = [onehot(row == ex[j : j + 1, :]) for j in range(SEND)]
    vals = [split_hl(ret_ref[pl.ds(j, nb, stride=SEND), :]) for j in range(SEND)]
    landed = fold(mm(jnp.concatenate(hots, axis=1), jnp.concatenate(vals, axis=0)))
    slot = lax.broadcasted_iota(jnp.int32, (slots, LANES), 0)
    out_ref[...] = jnp.where(slot < cnt_ref[0], part_ref[...] + landed, 0.0)


def call(
    kernel, out_shape, n_in, scalars=0, scratch=(), n_out=1, far=(), flops=10**8, moved=10**6
):
    vmem = pl.BlockSpec(memory_space=pltpu.VMEM)
    smem = pl.BlockSpec(memory_space=pltpu.SMEM)
    hbm = pl.BlockSpec(memory_space=pltpu.HBM)
    specs = [smem] * scalars + [vmem] * (n_in - scalars + n_out)
    shapes = list(out_shape) if n_out > 1 else [out_shape]
    for place in far:
        specs[place] = hbm
        if place >= n_in:
            old = shapes[place - n_in]
            shapes[place - n_in] = pltpu.HBM(old.shape, old.dtype)
    made = pl.pallas_call(
        kernel,
        out_shape=shapes if n_out > 1 else shapes[0],
        in_specs=specs[:n_in],
        out_specs=specs[n_in:] if n_out > 1 else specs[n_in],
        scratch_shapes=list(scratch),
        compiler_params=pltpu.CompilerParams(vmem_limit_bytes=VMEM_LIMIT),
        cost_estimate=pl.CostEstimate(flops=flops, bytes_accessed=moved, transcendentals=0),
    )

    def run(*args):
        placed = [
            pltpu.with_memory_space_constraint(x, pltpu.HBM) if i in far else x
            for i, x in enumerate(args)
        ]
        return made(*placed)

    return run


def sds(shape, dtype=F32):
    return jax.ShapeDtypeStruct(shape, dtype)


def across_chips(keep, give, later):
    nb = lax.axis_size("box")
    got = lax.ppermute(give, "box", [(i, i ^ 1) for i in range(nb)])
    both, later = lax.optimization_barrier((jnp.concatenate([keep, got], axis=1), later))
    groups = [[2 * chip + k for chip in chip_ranks(nb // 2)] for k in range(2)]
    landed = lax.all_to_all(
        both, "box", split_axis=0, concat_axis=0, axis_index_groups=groups, tiled=True
    )
    return landed.reshape(nb * SEND, LANES), later


def on_device(
    multipoles, parent_locals, box_counts, box_ids, pair_source, export_slots, operators, shifters
):
    coeffs, slots = multipoles.shape
    classes = operators.shape[0]
    nb = export_slots.shape[0]
    quarters = lax.axis_size("rep")
    quarter = slots // quarters
    sent = nb * SEND
    columns = slots + sent
    heavy = 2 * classes * slots * 2 * LANES * (columns + 2 * LANES)
    ex = export_slots.T
    core = (lax.axis_index("box") & 1).astype(jnp.int32).reshape(1)
    rep = lax.axis_index("rep").astype(jnp.int32).reshape(1)
    row = sds((slots, LANES))
    half = sds((nb // 2, SEND, LANES))
    wide = (classes, LANES, 2 * LANES)
    keep, give, mrow = call(
        export_kernel,
        [half, half, row],
        3,
        scalars=1,
        n_out=3,
        far=(1, 2),
        scratch=[
            pltpu.VMEM(multipoles.shape, F32),
            pltpu.VMEM(ex.shape, jnp.int32),
            pltpu.VMEM((sent, LANES), F32),
            pltpu.SemaphoreType.DMA,
            pltpu.SemaphoreType.DMA,
        ],
    )(core, multipoles, ex)
    arrived, mrow = across_chips(keep, give, mrow)
    w, own, keep, give = call(
        reverse_kernel,
        [sds(wide, BF), row, half, half],
        4,
        scalars=1,
        scratch=[
            pltpu.VMEM(operators.shape, F32),
            pltpu.VMEM((classes * LANES, LANES), F32),
            pltpu.VMEM(wide, BF),
            pltpu.VMEM((columns, 2 * LANES), F32),
            pltpu.SemaphoreType.DMA((classes // 8,)),
            pltpu.SemaphoreType.DMA,
        ],
        n_out=4,
        far=(1, 4),
        flops=heavy,
        moved=4 * operators.size,
    )(core, operators, mrow, pair_source)
    returned, own = across_chips(keep, give, own)
    part = call(
        forward_kernel,
        row,
        10,
        scalars=2,
        far=(2,),
        scratch=[
            pltpu.VMEM(wide, BF),
            pltpu.VMEM((columns, 2 * LANES), BF),
            pltpu.VMEM((classes, slots, LANES), jnp.int32),
            pltpu.VMEM((8 * LANES, LANES), F32),
            pltpu.VMEM((slots, 2 * LANES), F32),
            pltpu.SemaphoreType.DMA,
        ],
        flops=heavy,
        moved=4 * operators.size,
    )(rep, core, w, mrow, arrived, pair_source, box_ids.reshape(1, slots), parent_locals.T, shifters, own)
    summed = call(landing_kernel, row, 5, scalars=2)(core, box_counts, ex, returned, part)
    shares = lax.all_to_all(
        summed.reshape(quarters, quarter, LANES), "rep", split_axis=0, concat_axis=0, tiled=True
    )
    return jnp.sum(shares, axis=0)[:, :coeffs].T


def solution(mesh):
    return jax.shard_map(
        on_device,
        mesh=mesh,
        in_specs=(
            P(None, "box"),
            P(None, ("box", "rep")),
            P("box"),
            P("box"),
            P("rep", "box"),
            P("box", "rep"),
            P("rep", None),
            P(),
        ),
        out_specs=P(None, ("box", "rep")),
        check_vma=False,
    )
```

time: 244 us -> 81.1 us (0.33)
  the two profiles are of different devices: /device:TPU:40 before, /device:TPU:8 now
where the time goes in v1:
time: 81.1 us; the launch traced here: 80.7 us
  starting transfers between devices  29.4 us (36%)
  Pallas kernels  24.8 us (31%)
  waiting for transfers between devices  13.2 us (16%)
  blocking collectives  10.1 us (12%)
  other arithmetic  1.68 us (2%)
    all_to_all x2, starting transfers between devices, across_chips(): lax.all_to_all(both, 'box', split_axis=0, concat_axis=0, axis_index_group...  25.5 us
    pallas_call x4, Pallas kernels, run(): return made(*placed)  24.8 us
    all_to_all x2, waiting for transfers between devices, across_chips(): lax.all_to_all(both, 'box', split_axis=0, concat_axis=0, axis_index_group...  10.2 us
    all_to_all x1, blocking collectives, on_device(): lax.all_to_all(summed.reshape(quarters, quarter, LANES), 'rep', split_axi...  10.1 us
    ppermute x2, starting transfers between devices, across_chips(): got = lax.ppermute(give, 'box', [(i, i ^ 1) for i in range(nb)])  3.97 us
    ppermute x2, waiting for transfers between devices, across_chips(): got = lax.ppermute(give, 'box', [(i, i ^ 1) for i in range(nb)])  3 us
    concatenate x2, other arithmetic, across_chips(): jnp.concatenate([keep, got], axis=1)  1.67 us
  transfers between devices with their start and end apart: 4, of which 4 were waited for; matrix products, arithmetic and copies ran while one was open for 1% of the time, Pallas kernels for 28%

profile of v1, /device:TPU:8, one launch (start us, length us, event | category | flops | bytes accessed | tf_op | source)
XLA Modules:
  0.0 80.7 jit_solution(1919200413412535228)
XLA Ops:
  0.0 0.0 copy-start.2
  0.0 1.5 %shard_map.82 = (f32[64,8,128]{2,1,0:T(8,128)S(1)}, f32[64,8,128]{2,1,0:T(8,128)S(1)}, f32[256,128]{1,0:T(8,128)S(1)}) custom-call(s32[1]{0:T(128)} %bitcast.core_ref, f32[121,256]{1,0:T(8,128)} %mult_in.1, s32[8,128]{1,0:T(8,128)} %bitcast.13), custom_call_target="tpu_custom_call" | custom-call | flops 100000000 | bytes 1000000 | tf_op jit(solution)/shard_map/pallas_call | solution.py:313
  1.5 1.9 %collective-permute-start = (f32[64,8,128]{2,1,0:T(8,128)S(1)}, f32[64,8,128]{2,1,0:T(8,128)S(1)}, u32[]{:S(2)}, u32[]{:S(2)}) collective-permute-start(f32[64,8,128]{2,1,0:T(8,128)S(1)} %get-tuple-element.17), channel_id=1, source_target_pairs={{0,4},{4,0},{8,12},{12,8},{16,20},{20,16},{24,28},{28,24},{32,36},... | collective-permute-start | bytes 786440 | tf_op jit(solution)/shard_map/ppermute | solution.py:324
  3.4 1.5 %collective-permute-done = f32[64,8,128]{2,1,0:T(8,128)S(1)} collective-permute-done((f32[64,8,128]{2,1,0:T(8,128)S(1)}, f32[64,8,128]{2,1,0:T(8,128)S(1)}, u32[]{:S(2)}, u32[]{:S(2)}) %collective-permute-start) | collective-permute-done | bytes 262176 | tf_op jit(solution)/shard_map/ppermute | solution.py:324
  4.9 0.8 %pad_maximum_fusion = f32[64,16,128]{2,1,0:T(8,128)} fusion(f32[64,8,128]{2,1,0:T(8,128)S(1)} %collective-permute-done, f32[64,8,128]{2,1,0:T(8,128)S(1)} %get-tuple-element.16), kind=kLoop, calls=%fused_computation | loop fusion | flops 131072 | bytes 1048576 | tf_op jit(solution)/shard_map/concatenate | solution.py:325
  5.8 16.6 %all-to-all-start.1 = ((f32[64,16,128]{2,1,0:T(8,128)}), f32[64,16,128]{2,1,0:T(8,128)S(1)}, u32[]{:S(2)}, u32[]{:S(2)}) async-start(f32[64,16,128]{2,1,0:T(8,128)} %pad_maximum_fusion), calls=%async_computation.1 | async-start | bytes 1048576 | tf_op jit(solution)/shard_map/all_to_all | solution.py:327
  22.4 0.0 copy-done.2
  22.4 11.0 %shard_map.83 = (bf16[32,128,256]{2,1,0:T(8,128)(2,1)}, f32[256,128]{1,0:T(8,128)S(1)}, f32[64,8,128]{2,1,0:T(8,128)S(1)}, f32[64,8,128]{2,1,0:T(8,128)S(1)}) custom-call(s32[1]{0:T(128)} %bitcast.core_ref, f32[32,14641]{1,0:T(8,128)} %op_in.1, f32[256,128]{1,0:T(8,128)S(1)} %get-tuple-element.19.mrow_ref, s32[32,256]{1,0:T(8,128)S(1)} %copy-done.2), custom_call_target="tpu_custom_call" | custom-call | flops 6442450944 | bytes 1874048 | tf_op jit(solution)/shard_map/pallas_call | solution.py:313
  33.4 0.0 copy-start.1
  33.4 0.0 copy-start.3
  33.4 0.0 copy-start.4
  33.4 2.1 %collective-permute-start.1 = (f32[64,8,128]{2,1,0:T(8,128)S(1)}, f32[64,8,128]{2,1,0:T(8,128)S(1)}, u32[]{:S(2)}, u32[]{:S(2)}) collective-permute-start(f32[64,8,128]{2,1,0:T(8,128)S(1)} %get-tuple-element.21), channel_id=1, source_target_pairs={{0,4},{4,0},{8,12},{12,8},{16,20},{20,16},{24,28},{28,24},{32,36},... | collective-permute-start | bytes 786440 | tf_op jit(solution)/shard_map/ppermute | solution.py:324
  35.5 1.5 %collective-permute-done.1 = f32[64,8,128]{2,1,0:T(8,128)S(1)} collective-permute-done((f32[64,8,128]{2,1,0:T(8,128)S(1)}, f32[64,8,128]{2,1,0:T(8,128)S(1)}, u32[]{:S(2)}, u32[]{:S(2)}) %collective-permute-start.1) | collective-permute-done | bytes 262176 | tf_op jit(solution)/shard_map/ppermute | solution.py:324
  37.0 0.8 %pad_maximum_fusion.1 = f32[64,16,128]{2,1,0:T(8,128)} fusion(f32[64,8,128]{2,1,0:T(8,128)S(1)} %collective-permute-done.1, f32[64,8,128]{2,1,0:T(8,128)S(1)} %get-tuple-element.20), kind=kLoop, calls=%fused_computation.1 | loop fusion | flops 131072 | bytes 1048576 | tf_op jit(solution)/shard_map/concatenate | solution.py:325
  37.8 3.7 %all-to-all-done.1 = f32[64,16,128]{2,1,0:T(8,128)S(1)} async-done(((f32[64,16,128]{2,1,0:T(8,128)}), f32[64,16,128]{2,1,0:T(8,128)S(1)}, u32[]{:S(2)}, u32[]{:S(2)}) %all-to-all-start.1) | async-done | bytes 524320 | tf_op jit(solution)/shard_map/all_to_all | solution.py:327
  41.5 8.9 %all-to-all-start = ((f32[64,16,128]{2,1,0:T(8,128)}), f32[64,16,128]{2,1,0:T(8,128)S(1)}, u32[]{:S(2)}, u32[]{:S(2)}) async-start(f32[64,16,128]{2,1,0:T(8,128)} %pad_maximum_fusion.1), calls=%async_computation | async-start | bytes 1048576 | tf_op jit(solution)/shard_map/all_to_all | solution.py:327
  51.0 0.0 copy-done.1
  51.0 0.0 copy-done.3
  51.1 0.0 copy-done.4
  51.1 0.0 copy-start
  51.1 11.9 %shard_map.84.part_ref = f32[256,128]{1,0:T(8,128)S(1)} custom-call(s32[1]{0:T(128)} %bitcast.3.rep_ref, s32[1]{0:T(128)} %bitcast.core_ref, bf16[32,128,256]{2,1,0:T(8,128)(2,1)} %get-tuple-element.24.w_in, f32[256,128]{1,0:T(8,128)S(1)} %get-tuple-element.19.mrow_ref, f32[1024,128]{1,0:T(8,128)S(1)} %bitcast.11, s32[32,256]{1,0:T(8,128)S(1)} %copy-done.2, ...), custom_call_target="tpu_custom_call" | custom-call | flops 6442450944 | bytes 1874048 | tf_op jit(solution)/shard_map/pallas_call | solution.py:313
  63.0 6.5 %all-to-all-done = f32[64,16,128]{2,1,0:T(8,128)S(1)} async-done(((f32[64,16,128]{2,1,0:T(8,128)}), f32[64,16,128]{2,1,0:T(8,128)S(1)}, u32[]{:S(2)}, u32[]{:S(2)}) %all-to-all-start) | async-done | bytes 524320 | tf_op jit(solution)/shard_map/all_to_all | solution.py:327
  69.5 0.0 copy-done
  69.5 0.4 shard_map.85
  69.9 10.1 %all_to_all.15 = f32[4,64,128]{2,1,0:T(8,128)S(1)} all-to-all(f32[4,64,128]{2,1,0:T(8,128)S(1)} %bitcast.12), channel_id=1, replica_groups=mesh['box'=128,'rep'=4] {'rep'}, dimensions={0} | all-to-all | bytes 262144 | tf_op jit(solution)/shard_map/all_to_all | solution.py:403
  80.0 0.6 slice_bitcast_fusion
  (1 shorter events, 0.0 us)
Async XLA Ops:
  0.0 22.4 %copy-start.2 = (s32[32,256]{1,0:T(8,128)S(1)}, s32[32,256]{1,0:T(8,128)}, u32[]{:S(2)}) copy-start(s32[32,256]{1,0:T(8,128)} %ps_ref.3) | copy-start | bytes 98308
  1.5 3.4 %collective-permute-start = (f32[64,8,128]{2,1,0:T(8,128)S(1)}, f32[64,8,128]{2,1,0:T(8,128)S(1)}, u32[]{:S(2)}, u32[]{:S(2)}) collective-permute-start(f32[64,8,128]{2,1,0:T(8,128)S(1)} %get-tuple-element.17), channel_id=1, source_target_pairs={{0,4},{4,0},{8,12},{12,8},{16,20},{20,16},{24,28},{28,24},{32,36},... | collective-permute-start | bytes 786440 | tf_op jit(solution)/shard_map/ppermute | solution.py:324
  5.8 35.7 %all-to-all-start.1 = ((f32[64,16,128]{2,1,0:T(8,128)}), f32[64,16,128]{2,1,0:T(8,128)S(1)}, u32[]{:S(2)}, u32[]{:S(2)}) async-start(f32[64,16,128]{2,1,0:T(8,128)} %pad_maximum_fusion), calls=%async_computation.1 | async-start | bytes 1048576 | tf_op jit(solution)/shard_map/all_to_all | solution.py:327
  33.4 17.7 %copy-start.1 = (f32[8,14641]{1,0:T(8,128)S(1)}, f32[8,14641]{1,0:T(8,128)}, u32[]{:S(2)}) copy-start(f32[8,14641]{1,0:T(8,128)} %sh_ref.1) | copy-start | bytes 1405540
  33.4 17.7 %copy-start.3 = (f32[121,16]{0,1:T(8,128)S(1)}, f32[121,16]{0,1:T(8,128)}, u32[]{:S(2)}) copy-start(f32[121,16]{0,1:T(8,128)} %param.9) | copy-start | bytes 23236
  33.4 17.7 %copy-start.4 = (s32[256]{0:T(256)S(1)}, s32[256]{0:T(256)}, u32[]{:S(2)}) copy-start(s32[256]{0:T(256)} %param.11) | copy-start | bytes 3076
  33.4 3.6 %collective-permute-start.1 = (f32[64,8,128]{2,1,0:T(8,128)S(1)}, f32[64,8,128]{2,1,0:T(8,128)S(1)}, u32[]{:S(2)}, u32[]{:S(2)}) collective-permute-start(f32[64,8,128]{2,1,0:T(8,128)S(1)} %get-tuple-element.21), channel_id=1, source_target_pairs={{0,4},{4,0},{8,12},{12,8},{16,20},{20,16},{24,28},{28,24},{32,36},... | collective-permute-start | bytes 786440 | tf_op jit(solution)/shard_map/ppermute | solution.py:324
  41.5 28.0 %all-to-all-start = ((f32[64,16,128]{2,1,0:T(8,128)}), f32[64,16,128]{2,1,0:T(8,128)S(1)}, u32[]{:S(2)}, u32[]{:S(2)}) async-start(f32[64,16,128]{2,1,0:T(8,128)} %pad_maximum_fusion.1), calls=%async_computation | async-start | bytes 1048576 | tf_op jit(solution)/shard_map/all_to_all | solution.py:327
  51.1 18.4 %copy-start = (s32[128,8]{0,1:T(8,128)S(1)}, s32[128,8]{0,1:T(8,128)}, u32[]{:S(2)}) copy-start(s32[128,8]{0,1:T(8,128)} %param.13) | copy-start | bytes 12292

commit v2 on v1

--- a/solution.py
+++ b/solution.py
@@ -8,7 +8,6 @@
 ORDER = 10
 SEND = 8
 Z_BITS = 3
-Z_CHIPS = 1 << Z_BITS
 LANES = 128
 BF = jnp.bfloat16
 F32 = jnp.float32
@@ -60,33 +59,20 @@
         out[pl.ds(first * LANES + j, 8, stride=LANES), :] = jnp.zeros((8, LANES), F32)
 
 
-def chip_ranks(chips):
-    rows = chips // Z_CHIPS
-    return [((r // Z_CHIPS + r) % Z_CHIPS % rows) * Z_CHIPS + r % Z_CHIPS for r in range(chips)]
-
-
-def rank_columns(ex, core):
+def chip_side(chip):
+    return (chip ^ (chip >> Z_BITS)) & 1
+
+
+def swap_cores(ex, group):
     nb = ex.shape[1]
-    rows = nb // 2 // Z_CHIPS
-    source = lax.broadcasted_iota(jnp.int32, (nb, nb), 0)
-    place = lax.broadcasted_iota(jnp.int32, (nb, nb), 1)
-    rank = place >> 1
-    z = rank & (Z_CHIPS - 1)
-    y = (lax.shift_right_logical(rank, Z_BITS) + z) & (rows - 1)
-    column = ((y * Z_CHIPS + z) << 1) | ((place & 1) ^ core)
-    wide = jnp.concatenate([ex, ex], axis=0).astype(F32).astype(BF)
-    return mm(wide, onehot(source == column))[: ex.shape[0]].astype(jnp.int32)
-
-
-def far_order(ps, slots, nb, core):
-    rows = nb // 2 // Z_CHIPS
-    entry = ps - slots
-    peer = entry >> 3
-    z = (peer >> 1) & (Z_CHIPS - 1)
-    y = peer >> (1 + Z_BITS)
-    rank = ((y - z) & (rows - 1)) * Z_CHIPS + z
-    moved = (((rank << 1) | ((peer & 1) ^ core)) << 3) | (entry & (SEND - 1))
-    return jnp.where((entry >= 0) & (entry < nb * SEND), slots + moved, ps)
+    lane = lax.broadcasted_iota(jnp.int32, ex.shape, 1)
+    swapped = jnp.where((lane & 1) == 0, pltpu.roll(ex, nb - 1, 1), pltpu.roll(ex, 1, 1))
+    return jnp.where((chip_side(lane >> 1) ^ group) == 1, swapped, ex)
+
+
+def far_order(ps, slots, group):
+    swapped = chip_side((ps - slots) >> 4) ^ group
+    return ps ^ jnp.where(ps >= slots, SEND * swapped, 0)
 
 
 def spread_rows(row, rows):
@@ -99,7 +85,7 @@
 
 
 def export_kernel(
-    core_ref, mult_in, ex_in, keep_ref, give_ref, mrow_ref, mult_ref, ex_ref, all_ref, mult_sem, ex_sem
+    mult_in, ex_in, out, mrow_ref, mult_ref, ex_ref, cols_ref, sent_ref, mult_sem, ex_sem, out_sem
 ):
     fetch_mult = pltpu.make_async_copy(mult_in, mult_ref, mult_sem)
     fetch_ex = pltpu.make_async_copy(ex_in, ex_ref, ex_sem)
@@ -108,24 +94,31 @@
     fetch_ex.wait()
     coeffs, slots = mult_ref.shape
     nb = ex_ref.shape[1]
-    ex = rank_columns(ex_ref[...], core_ref[0])
-    ex = jnp.concatenate([ex, jnp.zeros((LANES - SEND, nb), jnp.int32)], axis=0).T
+    sent = nb * SEND
+    ex = jnp.concatenate([ex_ref[...], jnp.zeros((LANES - SEND, nb), jnp.int32)], axis=0).T
+    for j in range(SEND):
+        cols_ref[pl.ds(j, nb, stride=SEND), :] = jnp.broadcast_to(ex[:, j : j + 1], (nb, LANES))
     fetch_mult.wait()
     wide = jnp.concatenate([mult_ref[...], jnp.zeros((LANES - coeffs, slots), F32)], axis=0)
     rows = wide.T
     mrow_ref[...] = rows
     table = split_hl(rows)
-    lane = lax.broadcasted_iota(jnp.int32, (nb, slots), 1)
-    for j in range(SEND):
-        picked = mm(onehot(lane == ex[:, j : j + 1]), table)
-        all_ref[pl.ds(j, nb, stride=SEND), :] = fold(picked)
-    pairs = all_ref[...].reshape(nb // 2, 2 * SEND, LANES)
-    keep_ref[...] = pairs[:, :SEND, :]
-    give_ref[...] = pairs[:, SEND:, :]
+    block = 256
+    lane = lax.broadcasted_iota(jnp.int32, (block, LANES), 1)
+    copies = []
+    for n in range(sent // block):
+        here = pl.ds(n * block, block)
+        col = cols_ref[here, :]
+        hot = jnp.concatenate([onehot(lane == col - s) for s in range(0, slots, LANES)], axis=1)
+        sent_ref[here, :] = fold(mm(hot, table))
+        copies.append(pltpu.make_async_copy(sent_ref.at[here, :], out.at[here, :], out_sem.at[n]))
+        copies[n].start()
+    for copy in copies:
+        copy.wait()
 
 
 def reverse_kernel(
-    core_ref,
+    group_ref,
     op_in,
     mrow_ref,
     ps_ref,
@@ -144,7 +137,7 @@
     coeffs = 121
     slots = mrow_ref.shape[0]
     columns = acc_ref.shape[0]
-    group = 8
+    step = 8
     block = 256
 
     def fetch(k):
@@ -164,21 +157,21 @@
     acc_ref[...] = jnp.zeros_like(acc_ref)
     row_id = lax.broadcasted_iota(jnp.int32, (block, slots), 0).astype(F32).astype(BF)
 
-    @pl.loop(0, classes // group)
+    @pl.loop(0, classes // step)
     def _(g):
         mirrors = []
-        for i in range(group):
-            c = g * group + i
+        for i in range(step):
+            c = g * step + i
             w = split_hl(t_ref[pl.ds(pl.multiple_of(c * LANES, LANES), LANES), :].T)
             w_ref[c] = w
             mirrors.append(split_hl(fold(mm(moments, jnp.concatenate([w, w], axis=0)))))
         m = jnp.concatenate(mirrors, axis=0)
-        ps = ps_ref[pl.ds(pl.multiple_of(g * group, group), group), :]
-        ps = far_order(ps, slots, (columns - slots) // SEND, core_ref[0])
+        ps = ps_ref[pl.ds(pl.multiple_of(g * step, step), step), :]
+        ps = far_order(ps, slots, group_ref[0])
         for start in range(0, columns, block):
             here = ps - start
             hot = jnp.concatenate(
-                [pick16(row_id == spread_rows(here[i : i + 1, :], block)) for i in range(group)],
+                [pick16(row_id == spread_rows(here[i : i + 1, :], block)) for i in range(step)],
                 axis=1,
             )
             acc_ref[start : start + block, :] += mm(hot, m)
@@ -196,7 +189,6 @@
 
 def forward_kernel(
     rep_ref,
-    core_ref,
     w_in,
     mrow_ref,
     arr_ref,
@@ -222,7 +214,7 @@
     block = 256
     table_ref[:slots, :] = split_hl(mrow_ref[...])
     table_ref[slots:, :] = split_hl(arr_ref[...])
-    ps = far_order(ps_ref[...], slots, (columns - slots) // SEND, core_ref[0])
+    ps = ps_ref[...]
     pst = jnp.concatenate([ps, jnp.zeros((LANES - classes, slots), jnp.int32)], axis=0).T
     for c in range(classes):
         cols_ref[c] = jnp.broadcast_to(pst[:, c : c + 1], (slots, LANES))
@@ -270,11 +262,11 @@
     out_ref[...] = fold(acc_ref[...]) + own_ref[...] + shifted
 
 
-def landing_kernel(core_ref, cnt_ref, ex_ref, ret_ref, part_ref, out_ref):
+def landing_kernel(group_ref, cnt_ref, ex_ref, ret_ref, part_ref, out_ref):
     slots = part_ref.shape[0]
     nb = ex_ref.shape[1]
     row = lax.broadcasted_iota(jnp.int32, (slots, nb), 0)
-    ex = rank_columns(ex_ref[...], core_ref[0])
+    ex = swap_cores(ex_ref[...], group_ref[0])
     hots = [onehot(row == ex[j : j + 1, :]) for j in range(SEND)]
     vals = [split_hl(ret_ref[pl.ds(j, nb, stride=SEND), :]) for j in range(SEND)]
     landed = fold(mm(jnp.concatenate(hots, axis=1), jnp.concatenate(vals, axis=0)))
@@ -323,7 +315,7 @@
     nb = lax.axis_size("box")
     got = lax.ppermute(give, "box", [(i, i ^ 1) for i in range(nb)])
     both, later = lax.optimization_barrier((jnp.concatenate([keep, got], axis=1), later))
-    groups = [[2 * chip + k for chip in chip_ranks(nb // 2)] for k in range(2)]
+    groups = [[2 * chip + (chip_side(chip) ^ g) for chip in range(nb // 2)] for g in range(2)]
     landed = lax.all_to_all(
         both, "box", split_axis=0, concat_axis=0, axis_index_groups=groups, tiled=True
     )
@@ -342,27 +334,31 @@
     columns = slots + sent
     heavy = 2 * classes * slots * 2 * LANES * (columns + 2 * LANES)
     ex = export_slots.T
-    core = (lax.axis_index("box") & 1).astype(jnp.int32).reshape(1)
+    box = lax.axis_index("box").astype(jnp.int32)
+    group = ((box & 1) ^ chip_side(box >> 1)).reshape(1)
     rep = lax.axis_index("rep").astype(jnp.int32).reshape(1)
     row = sds((slots, LANES))
     half = sds((nb // 2, SEND, LANES))
     wide = (classes, LANES, 2 * LANES)
-    keep, give, mrow = call(
+    outgoing, mrow = call(
         export_kernel,
-        [half, half, row],
-        3,
-        scalars=1,
-        n_out=3,
-        far=(1, 2),
+        [sds((sent, LANES)), row],
+        2,
+        n_out=2,
+        far=(0, 1, 2),
         scratch=[
             pltpu.VMEM(multipoles.shape, F32),
             pltpu.VMEM(ex.shape, jnp.int32),
+            pltpu.VMEM((sent, LANES), jnp.int32),
             pltpu.VMEM((sent, LANES), F32),
             pltpu.SemaphoreType.DMA,
             pltpu.SemaphoreType.DMA,
+            pltpu.SemaphoreType.DMA((sent // 256,)),
         ],
-    )(core, multipoles, ex)
-    arrived, mrow = across_chips(keep, give, mrow)
+    )(multipoles, ex)
+    arrived = lax.all_to_all(
+        outgoing.reshape(nb, SEND, LANES), "box", split_axis=0, concat_axis=0, tiled=True
+    ).reshape(sent, LANES)
     w, own, keep, give = call(
         reverse_kernel,
         [sds(wide, BF), row, half, half],
@@ -380,14 +376,14 @@
         far=(1, 4),
         flops=heavy,
         moved=4 * operators.size,
-    )(core, operators, mrow, pair_source)
+    )(group, operators, mrow, pair_source)
     returned, own = across_chips(keep, give, own)
     part = call(
         forward_kernel,
         row,
-        10,
-        scalars=2,
-        far=(2,),
+        9,
+        scalars=1,
+        far=(1,),
         scratch=[
             pltpu.VMEM(wide, BF),
             pltpu.VMEM((columns, 2 * LANES), BF),
@@ -398,8 +394,8 @@
         ],
         flops=heavy,
         moved=4 * operators.size,
-    )(rep, core, w, mrow, arrived, pair_source, box_ids.reshape(1, slots), parent_locals.T, shifters, own)
-    summed = call(landing_kernel, row, 5, scalars=2)(core, box_counts, ex, returned, part)
+    )(rep, w, mrow, arrived, pair_source, box_ids.reshape(1, slots), parent_locals.T, shifters, own)
+    summed = call(landing_kernel, row, 5, scalars=2)(group, box_counts, ex, returned, part)
     shares = lax.all_to_all(
         summed.reshape(quarters, quarter, LANES), "rep", split_axis=0, concat_axis=0, tiled=True
     )

time: 81.1 us -> 79.3 us (0.978)
  starting transfers between devices: 29.4 us -> 27.9 us
  waiting for transfers between devices: 13.2 us -> 12.3 us
    all_to_all x0 -> x1, starting transfers between devices: none -> 17.4 us  [on_device(): lax.all_to_all(outgoing.reshape(nb, SEND, LANES), 'box', split_axis=0, co...]
    all_to_all x2 -> x1, starting transfers between devices: 25.5 us -> 8.35 us  [across_chips(): lax.all_to_all(both, 'box', split_axis=0, concat_axis=0, axis_index_group...]
    all_to_all x0 -> x1, waiting for transfers between devices: none -> 4.06 us  [on_device(): lax.all_to_all(outgoing.reshape(nb, SEND, LANES), 'box', split_axis=0, co...]
    all_to_all x2 -> x1, waiting for transfers between devices: 10.2 us -> 6.86 us  [across_chips(): lax.all_to_all(both, 'box', split_axis=0, concat_axis=0, axis_index_group...]
    ppermute x2 -> x1, starting transfers between devices: 3.97 us -> 2.19 us  [across_chips(): got = lax.ppermute(give, 'box', [(i, i ^ 1) for i in range(nb)])]
    ppermute x2 -> x1, waiting for transfers between devices: 3 us -> 1.37 us  [across_chips(): got = lax.ppermute(give, 'box', [(i, i ^ 1) for i in range(nb)])]
    concatenate x2 -> x1, other arithmetic: 1.67 us -> 0.87 us  [across_chips(): jnp.concatenate([keep, got], axis=1)]
  transfers between devices with their start and end apart: 4 -> 3, of which waited for: 4 -> 3; matrix products, arithmetic and copies ran while one was open for 1% -> 1% of each run, Pallas kernels for 28% -> 29%
where the time goes in v2:
time: 79.3 us; the launch traced here: 78.9 us
  starting transfers between devices  27.9 us (35%)
  Pallas kernels  25.5 us (32%)
  waiting for transfers between devices  12.3 us (16%)
  blocking collectives  10.1 us (13%)
  local copies, waits for them, and re-layouts  1.4 us (2%)
  other arithmetic  0.88 us (1%)
  between operations  0.8 us (1%)
    pallas_call x4, Pallas kernels, run(): return made(*placed)  25.5 us
    all_to_all x1, starting transfers between devices, on_device(): lax.all_to_all(outgoing.reshape(nb, SEND, LANES), 'box', split_axis=0, co...  17.4 us
    all_to_all x1, blocking collectives, on_device(): lax.all_to_all(summed.reshape(quarters, quarter, LANES), 'rep', split_axi...  10.1 us
    all_to_all x1, starting transfers between devices, across_chips(): lax.all_to_all(both, 'box', split_axis=0, concat_axis=0, axis_index_group...  8.35 us
    all_to_all x1, waiting for transfers between devices, across_chips(): lax.all_to_all(both, 'box', split_axis=0, concat_axis=0, axis_index_group...  6.86 us
    all_to_all x1, waiting for transfers between devices, on_device(): lax.all_to_all(outgoing.reshape(nb, SEND, LANES), 'box', split_axis=0, co...  4.06 us
    ppermute x1, starting transfers between devices, across_chips(): got = lax.ppermute(give, 'box', [(i, i ^ 1) for i in range(nb)])  2.19 us
  transfers between devices with their start and end apart: 3, of which 3 were waited for; matrix products, arithmetic and copies ran while one was open for 1% of the time, Pallas kernels for 29%

profile of v2, /device:TPU:8, one launch (start us, length us, event | category | flops | bytes accessed | tf_op | source)
XLA Modules:
  0.0 78.9 jit_solution(15658476795875961765)
XLA Ops:
  0.0 2.3 %shard_map.82 = (f32[1024,128]{1,0:T(8,128)}, f32[256,128]{1,0:T(8,128)S(1)}) custom-call(f32[121,256]{1,0:T(8,128)} %mult_in.1, s32[8,128]{1,0:T(8,128)} %bitcast.14), custom_call_target="tpu_custom_call" | custom-call | flops 100000000 | bytes 1000000 | tf_op jit(solution)/shard_map/pallas_call | solution.py:305
  2.3 17.4 %all-to-all-start.1 = ((f32[128,8,128]{2,1,0:T(8,128)}), f32[128,8,128]{2,1,0:T(8,128)S(1)}, u32[]{:S(2)}, u32[]{:S(2)}) async-start(f32[128,8,128]{2,1,0:T(8,128)} %bitcast.18), calls=%async_computation.1 | async-start | bytes 1048576 | tf_op jit(solution)/shard_map/all_to_all | solution.py:359
  19.7 0.0 copy-start.2
  19.7 0.7 copy-done.2
  20.4 11.0 %shard_map.83 = (bf16[32,128,256]{2,1,0:T(8,128)(2,1)}, f32[256,128]{1,0:T(8,128)S(1)}, f32[64,8,128]{2,1,0:T(8,128)S(1)}, f32[64,8,128]{2,1,0:T(8,128)S(1)}) custom-call(s32[1]{0:T(128)} %bitcast.group_ref, f32[32,14641]{1,0:T(8,128)} %op_in.1, f32[256,128]{1,0:T(8,128)S(1)} %get-tuple-element.13.mrow_ref, s32[32,256]{1,0:T(8,128)S(1)} %copy-done.2), custom_call_target="tpu_custom_call" | custom-call | flops 6442450944 | bytes 1874048 | tf_op jit(solution)/shard_map/pallas_call | solution.py:305
  31.4 0.0 copy-start.1
  31.4 0.0 copy-start.3
  31.4 0.0 copy-start.4
  31.4 0.0 copy-start.5
  31.5 2.2 %collective-permute-start = (f32[64,8,128]{2,1,0:T(8,128)S(1)}, f32[64,8,128]{2,1,0:T(8,128)S(1)}, u32[]{:S(2)}, u32[]{:S(2)}) collective-permute-start(f32[64,8,128]{2,1,0:T(8,128)S(1)} %get-tuple-element.15), channel_id=1, source_target_pairs={{0,4},{4,0},{8,12},{12,8},{16,20},{20,16},{24,28},{28,24},{32,36},... | collective-permute-start | bytes 786440 | tf_op jit(solution)/shard_map/ppermute | solution.py:316
  33.7 1.4 %collective-permute-done = f32[64,8,128]{2,1,0:T(8,128)S(1)} collective-permute-done((f32[64,8,128]{2,1,0:T(8,128)S(1)}, f32[64,8,128]{2,1,0:T(8,128)S(1)}, u32[]{:S(2)}, u32[]{:S(2)}) %collective-permute-start) | collective-permute-done | bytes 262176 | tf_op jit(solution)/shard_map/ppermute | solution.py:316
  35.0 0.9 %pad_maximum_fusion = f32[64,16,128]{2,1,0:T(8,128)} fusion(f32[64,8,128]{2,1,0:T(8,128)S(1)} %collective-permute-done, f32[64,8,128]{2,1,0:T(8,128)S(1)} %get-tuple-element.14), kind=kLoop, calls=%fused_computation | loop fusion | flops 131072 | bytes 1048576 | tf_op jit(solution)/shard_map/concatenate | solution.py:317
  35.9 4.1 %all-to-all-done.1 = f32[128,8,128]{2,1,0:T(8,128)S(1)} async-done(((f32[128,8,128]{2,1,0:T(8,128)}), f32[128,8,128]{2,1,0:T(8,128)S(1)}, u32[]{:S(2)}, u32[]{:S(2)}) %all-to-all-start.1) | async-done | bytes 524320 | tf_op jit(solution)/shard_map/all_to_all | solution.py:359
  40.0 8.4 %all-to-all-start = ((f32[64,16,128]{2,1,0:T(8,128)}), f32[64,16,128]{2,1,0:T(8,128)S(1)}, u32[]{:S(2)}, u32[]{:S(2)}) async-start(f32[64,16,128]{2,1,0:T(8,128)} %pad_maximum_fusion), calls=%async_computation | async-start | bytes 1048576 | tf_op jit(solution)/shard_map/all_to_all | solution.py:319
  49.0 0.0 copy-done.1
  49.0 0.0 copy-done.3
  49.0 0.0 copy-done.4
  49.0 0.0 copy-done.5
  49.0 0.0 copy-start
  49.0 11.9 %shard_map.84.part_ref = f32[256,128]{1,0:T(8,128)S(1)} custom-call(s32[1]{0:T(128)} %bitcast.3.rep_ref, bf16[32,128,256]{2,1,0:T(8,128)(2,1)} %get-tuple-element.18.w_in, f32[256,128]{1,0:T(8,128)S(1)} %get-tuple-element.13.mrow_ref, f32[1024,128]{1,0:T(8,128)S(1)} %bitcast.12, s32[32,256]{1,0:T(8,128)S(1)} %copy-done.3, s32[1,256]{1,0:T(1,128)S(1)} %bitcast.17, ...), custom_call_target="tpu_custom_call" | custom-call | flops 6442450944 | bytes 1874048 | tf_op jit(solution)/shard_map/pallas_call | solution.py:305
  61.0 6.9 %all-to-all-done = f32[64,16,128]{2,1,0:T(8,128)S(1)} async-done(((f32[64,16,128]{2,1,0:T(8,128)}), f32[64,16,128]{2,1,0:T(8,128)S(1)}, u32[]{:S(2)}, u32[]{:S(2)}) %all-to-all-start) | async-done | bytes 524320 | tf_op jit(solution)/shard_map/all_to_all | solution.py:319
  67.8 0.0 copy-done
  67.8 0.4 shard_map.85
  68.2 10.1 %all_to_all.15 = f32[4,64,128]{2,1,0:T(8,128)S(1)} all-to-all(f32[4,64,128]{2,1,0:T(8,128)S(1)} %bitcast.13), channel_id=1, replica_groups=mesh['box'=128,'rep'=4] {'rep'}, dimensions={0} | all-to-all | bytes 262144 | tf_op jit(solution)/shard_map/all_to_all | solution.py:399
  78.3 0.6 slice_bitcast_fusion
  (1 shorter events, 0.0 us)
Async XLA Ops:
  2.3 37.7 %all-to-all-start.1 = ((f32[128,8,128]{2,1,0:T(8,128)}), f32[128,8,128]{2,1,0:T(8,128)S(1)}, u32[]{:S(2)}, u32[]{:S(2)}) async-start(f32[128,8,128]{2,1,0:T(8,128)} %bitcast.18), calls=%async_computation.1 | async-start | bytes 1048576 | tf_op jit(solution)/shard_map/all_to_all | solution.py:359
  19.7 0.8 copy-start.2
  31.4 17.6 %copy-start.1 = (f32[8,14641]{1,0:T(8,128)S(1)}, f32[8,14641]{1,0:T(8,128)}, u32[]{:S(2)}) copy-start(f32[8,14641]{1,0:T(8,128)} %sh_ref.1) | copy-start | bytes 1405540
  31.4 17.6 %copy-start.3 = (s32[32,256]{1,0:T(8,128)S(1)}, s32[32,256]{1,0:T(8,128)}, u32[]{:S(2)}) copy-start(s32[32,256]{1,0:T(8,128)} %ps_ref.3) | copy-start | bytes 98308
  31.4 17.6 %copy-start.4 = (f32[121,16]{0,1:T(8,128)S(1)}, f32[121,16]{0,1:T(8,128)}, u32[]{:S(2)}) copy-start(f32[121,16]{0,1:T(8,128)} %param.9) | copy-start | bytes 23236
  31.4 17.6 %copy-start.5 = (s32[256]{0:T(256)S(1)}, s32[256]{0:T(256)}, u32[]{:S(2)}) copy-start(s32[256]{0:T(256)} %param.11) | copy-start | bytes 3076
  31.5 3.6 %collective-permute-start = (f32[64,8,128]{2,1,0:T(8,128)S(1)}, f32[64,8,128]{2,1,0:T(8,128)S(1)}, u32[]{:S(2)}, u32[]{:S(2)}) collective-permute-start(f32[64,8,128]{2,1,0:T(8,128)S(1)} %get-tuple-element.15), channel_id=1, source_target_pairs={{0,4},{4,0},{8,12},{12,8},{16,20},{20,16},{24,28},{28,24},{32,36},... | collective-permute-start | bytes 786440 | tf_op jit(solution)/shard_map/ppermute | solution.py:316
  40.0 27.9 %all-to-all-start = ((f32[64,16,128]{2,1,0:T(8,128)}), f32[64,16,128]{2,1,0:T(8,128)S(1)}, u32[]{:S(2)}, u32[]{:S(2)}) async-start(f32[64,16,128]{2,1,0:T(8,128)} %pad_maximum_fusion), calls=%async_computation | async-start | bytes 1048576 | tf_op jit(solution)/shard_map/all_to_all | solution.py:319
  49.0 18.8 %copy-start = (s32[128,8]{0,1:T(8,128)S(1)}, s32[128,8]{0,1:T(8,128)}, u32[]{:S(2)}) copy-start(s32[128,8]{0,1:T(8,128)} %param.13) | copy-start | bytes 12292

commit v3 on v2

--- a/solution.py
+++ b/solution.py
@@ -85,7 +85,7 @@
 
 
 def export_kernel(
-    mult_in, ex_in, out, mrow_ref, mult_ref, ex_ref, cols_ref, sent_ref, mult_sem, ex_sem, out_sem
+    mult_in, ex_in, sent_ref, mrow_ref, mult_ref, ex_ref, cols_ref, mult_sem, ex_sem
 ):
     fetch_mult = pltpu.make_async_copy(mult_in, mult_ref, mult_sem)
     fetch_ex = pltpu.make_async_copy(ex_in, ex_ref, ex_sem)
@@ -105,32 +105,31 @@
     table = split_hl(rows)
     block = 256
     lane = lax.broadcasted_iota(jnp.int32, (block, LANES), 1)
-    copies = []
     for n in range(sent // block):
         here = pl.ds(n * block, block)
         col = cols_ref[here, :]
         hot = jnp.concatenate([onehot(lane == col - s) for s in range(0, slots, LANES)], axis=1)
         sent_ref[here, :] = fold(mm(hot, table))
-        copies.append(pltpu.make_async_copy(sent_ref.at[here, :], out.at[here, :], out_sem.at[n]))
-        copies[n].start()
-    for copy in copies:
-        copy.wait()
 
 
 def reverse_kernel(
     group_ref,
     op_in,
     mrow_ref,
-    ps_ref,
+    ps_in,
     w_out,
     own_ref,
     keep_ref,
     give_ref,
     op_ref,
+    ps_ref,
     t_ref,
     w_ref,
+    m_even,
+    m_odd,
     acc_ref,
     op_sem,
+    ps_sem,
     w_sem,
 ):
     classes = op_ref.shape[0]
@@ -146,28 +145,30 @@
 
     for k in range(classes // 8):
         fetch(k).start()
-
-    @pl.loop(0, classes // 8)
-    def _(k):
-        fetch(k).wait()
-        matrices_to_rows(op_ref, pl.multiple_of(k * 8, 8), coeffs, t_ref)
+    fetch_ps = pltpu.make_async_copy(ps_in, ps_ref, ps_sem)
+    fetch_ps.start()
+
+    def keep_w(g):
+        part = pl.ds(g * step, step)
+        return pltpu.make_async_copy(w_ref.at[part], w_out.at[part], w_sem.at[g])
 
     sign = parity_lanes(slots)
     moments = split_hl(mrow_ref[...] * sign)
     acc_ref[...] = jnp.zeros_like(acc_ref)
     row_id = lax.broadcasted_iota(jnp.int32, (block, slots), 0).astype(F32).astype(BF)
 
-    @pl.loop(0, classes // step)
-    def _(g):
-        mirrors = []
+    def prepare(g, out):
+        matrices_to_rows(op_ref, g * step, coeffs, t_ref)
         for i in range(step):
             c = g * step + i
-            w = split_hl(t_ref[pl.ds(pl.multiple_of(c * LANES, LANES), LANES), :].T)
+            w = split_hl(t_ref[c * LANES : (c + 1) * LANES, :].T)
             w_ref[c] = w
-            mirrors.append(split_hl(fold(mm(moments, jnp.concatenate([w, w], axis=0)))))
-        m = jnp.concatenate(mirrors, axis=0)
-        ps = ps_ref[pl.ds(pl.multiple_of(g * step, step), step), :]
-        ps = far_order(ps, slots, group_ref[0])
+            mirrored = fold(mm(moments, jnp.concatenate([w, w], axis=0)))
+            out[i * slots : (i + 1) * slots, :] = split_hl(mirrored)
+
+    def scatter(g, held):
+        m = held[...]
+        ps = far_order(ps_ref[g * step : (g + 1) * step, :], slots, group_ref[0])
         for start in range(0, columns, block):
             here = ps - start
             hot = jnp.concatenate(
@@ -176,15 +177,27 @@
             )
             acc_ref[start : start + block, :] += mm(hot, m)
 
-    copy = pltpu.make_async_copy(w_ref, w_out, w_sem)
-    copy.start()
+    groups = classes // step
+    held = (m_even, m_odd)
+    fetch(0).wait()
+    prepare(0, held[0])
+    fetch_ps.wait()
+    for g in range(1, groups):
+        fetch(g).wait()
+    for g in range(groups):
+        keep_w(g).start()
+        if g + 1 < groups:
+            prepare(g + 1, held[(g + 1) % 2])
+        scatter(g, held[g % 2])
+
     own_ref[...] = fold(acc_ref[:slots, :]) * sign
     far = columns - slots
     sums = fold(acc_ref[slots:, :]) * parity_lanes(far)
     pairs = sums.reshape(far // (2 * SEND), 2 * SEND, LANES)
     keep_ref[...] = pairs[:, :SEND, :]
     give_ref[...] = pairs[:, SEND:, :]
-    copy.wait()
+    for g in range(classes // step):
+        keep_w(g).wait()
 
 
 def forward_kernel(
@@ -275,7 +288,7 @@
 
 
 def call(
-    kernel, out_shape, n_in, scalars=0, scratch=(), n_out=1, far=(), flops=10**8, moved=10**6
+    kernel, out_shape, n_in, scalars=0, scratch=(), n_out=1, far=(), near=(), flops=10**8, moved=10**6
 ):
     vmem = pl.BlockSpec(memory_space=pltpu.VMEM)
     smem = pl.BlockSpec(memory_space=pltpu.SMEM)
@@ -287,6 +300,9 @@
         if place >= n_in:
             old = shapes[place - n_in]
             shapes[place - n_in] = pltpu.HBM(old.shape, old.dtype)
+    for place in near:
+        old = shapes[place - n_in]
+        shapes[place - n_in] = pltpu.VMEM(old.shape, old.dtype)
     made = pl.pallas_call(
         kernel,
         out_shape=shapes if n_out > 1 else shapes[0],
@@ -345,15 +361,14 @@
         [sds((sent, LANES)), row],
         2,
         n_out=2,
-        far=(0, 1, 2),
+        far=(0, 1),
+        near=(2,),
         scratch=[
             pltpu.VMEM(multipoles.shape, F32),
             pltpu.VMEM(ex.shape, jnp.int32),
             pltpu.VMEM((sent, LANES), jnp.int32),
-            pltpu.VMEM((sent, LANES), F32),
             pltpu.SemaphoreType.DMA,
             pltpu.SemaphoreType.DMA,
-            pltpu.SemaphoreType.DMA((sent // 256,)),
         ],
     )(multipoles, ex)
     arrived = lax.all_to_all(
@@ -366,14 +381,18 @@
         scalars=1,
         scratch=[
             pltpu.VMEM(operators.shape, F32),
+            pltpu.VMEM((classes, slots), jnp.int32),
             pltpu.VMEM((classes * LANES, LANES), F32),
             pltpu.VMEM(wide, BF),
+            pltpu.VMEM((8 * slots, 2 * LANES), BF),
+            pltpu.VMEM((8 * slots, 2 * LANES), BF),
             pltpu.VMEM((columns, 2 * LANES), F32),
             pltpu.SemaphoreType.DMA((classes // 8,)),
             pltpu.SemaphoreType.DMA,
+            pltpu.SemaphoreType.DMA((classes // 8,)),
         ],
         n_out=4,
-        far=(1, 4),
+        far=(1, 3, 4),
         flops=heavy,
         moved=4 * operators.size,
     )(group, operators, mrow, pair_source)

time: 79.3 us -> 76.8 us (0.968)
  starting transfers between devices: 27.9 us -> 25.4 us
  waiting for transfers between devices: 12.3 us -> 14.8 us
  Pallas kernels: 25.5 us -> 23.8 us
    all_to_all x1, waiting for transfers between devices: 4.06 us -> 6.56 us  [on_device(): lax.all_to_all(outgoing.reshape(nb, SEND, LANES), 'box', split_axis=0, co...]
    all_to_all x1, starting transfers between devices: 8.35 us -> 5.87 us  [across_chips(): lax.all_to_all(both, 'box', split_axis=0, concat_axis=0, axis_index_group...]
    pallas_call x4, Pallas kernels: 25.5 us -> 23.8 us  [run(): return made(*placed)]
  transfers between devices with their start and end apart: 3 -> 3, of which waited for: 3 -> 3; matrix products, arithmetic and copies ran while one was open for 1% -> 1% of each run, Pallas kernels for 29% -> 28%
where the time goes in v3:
time: 76.8 us; the launch traced here: 76.4 us
  starting transfers between devices  25.4 us (33%)
  Pallas kernels  23.8 us (31%)
  waiting for transfers between devices  14.8 us (19%)
  blocking collectives  10.1 us (13%)
  other arithmetic  0.85 us (1%)
  between operations  0.79 us (1%)
    pallas_call x4, Pallas kernels, run(): return made(*placed)  23.8 us
    all_to_all x1, starting transfers between devices, on_device(): lax.all_to_all(outgoing.reshape(nb, SEND, LANES), 'box', split_axis=0, co...  17.4 us
    all_to_all x1, blocking collectives, on_device(): lax.all_to_all(summed.reshape(quarters, quarter, LANES), 'rep', split_axi...  10.1 us
    all_to_all x1, waiting for transfers between devices, across_chips(): lax.all_to_all(both, 'box', split_axis=0, concat_axis=0, axis_index_group...  6.84 us
    all_to_all x1, waiting for transfers between devices, on_device(): lax.all_to_all(outgoing.reshape(nb, SEND, LANES), 'box', split_axis=0, co...  6.56 us
    all_to_all x1, starting transfers between devices, across_chips(): lax.all_to_all(both, 'box', split_axis=0, concat_axis=0, axis_index_group...  5.87 us
    ppermute x1, starting transfers between devices, across_chips(): got = lax.ppermute(give, 'box', [(i, i ^ 1) for i in range(nb)])  2.19 us
  transfers between devices with their start and end apart: 3, of which 3 were waited for; matrix products, arithmetic and copies ran while one was open for 1% of the time, Pallas kernels for 28%

profile of v3, /device:TPU:8, one launch (start us, length us, event | category | flops | bytes accessed | tf_op | source)
XLA Modules:
  0.0 76.4 jit_solution(9329194206525976261)
XLA Ops:
  0.0 2.3 %shard_map.82 = (f32[1024,128]{1,0:T(8,128)}, f32[256,128]{1,0:T(8,128)S(1)}) custom-call(f32[121,256]{1,0:T(8,128)} %mult_in.1, s32[8,128]{1,0:T(8,128)} %bitcast.14), custom_call_target="tpu_custom_call" | custom-call | flops 100000000 | bytes 1000000 | tf_op jit(solution)/shard_map/pallas_call | solution.py:321
  2.3 17.4 %all-to-all-start.1 = ((f32[128,8,128]{2,1,0:T(8,128)}), f32[128,8,128]{2,1,0:T(8,128)S(1)}, u32[]{:S(2)}, u32[]{:S(2)}) async-start(f32[128,8,128]{2,1,0:T(8,128)} %bitcast.4), calls=%async_computation.1 | async-start | bytes 1048576 | tf_op jit(solution)/shard_map/all_to_all | solution.py:374
  19.7 9.3 %shard_map.83 = (bf16[32,128,256]{2,1,0:T(8,128)(2,1)}, f32[256,128]{1,0:T(8,128)S(1)}, f32[64,8,128]{2,1,0:T(8,128)S(1)}, f32[64,8,128]{2,1,0:T(8,128)S(1)}) custom-call(s32[1]{0:T(128)} %bitcast.group_ref, f32[32,14641]{1,0:T(8,128)} %op_in.1, f32[256,128]{1,0:T(8,128)S(1)} %get-tuple-element.13.mrow_ref, s32[32,256]{1,0:T(8,128)} %ps_ref.1), custom_call_target="tpu_custom_call" | custom-call | flops 6442450944 | bytes 1874048 | tf_op jit(solution)/shard_map/pallas_call | solution.py:321
  29.0 0.0 copy-start.1
  29.0 0.0 copy-start.2
  29.0 0.0 copy-start.3
  29.0 0.0 copy-start.4
  29.0 2.2 %collective-permute-start = (f32[64,8,128]{2,1,0:T(8,128)S(1)}, f32[64,8,128]{2,1,0:T(8,128)S(1)}, u32[]{:S(2)}, u32[]{:S(2)}) collective-permute-start(f32[64,8,128]{2,1,0:T(8,128)S(1)} %get-tuple-element.15), channel_id=1, source_target_pairs={{0,4},{4,0},{8,12},{12,8},{16,20},{20,16},{24,28},{28,24},{32,36},... | collective-permute-start | bytes 786440 | tf_op jit(solution)/shard_map/ppermute | solution.py:332
  31.2 1.4 %collective-permute-done = f32[64,8,128]{2,1,0:T(8,128)S(1)} collective-permute-done((f32[64,8,128]{2,1,0:T(8,128)S(1)}, f32[64,8,128]{2,1,0:T(8,128)S(1)}, u32[]{:S(2)}, u32[]{:S(2)}) %collective-permute-start) | collective-permute-done | bytes 262176 | tf_op jit(solution)/shard_map/ppermute | solution.py:332
  32.6 0.8 %pad_maximum_fusion = f32[64,16,128]{2,1,0:T(8,128)} fusion(f32[64,8,128]{2,1,0:T(8,128)S(1)} %collective-permute-done, f32[64,8,128]{2,1,0:T(8,128)S(1)} %get-tuple-element.14), kind=kLoop, calls=%fused_computation | loop fusion | flops 131072 | bytes 1048576 | tf_op jit(solution)/shard_map/concatenate | solution.py:333
  33.4 6.6 %all-to-all-done.1 = f32[128,8,128]{2,1,0:T(8,128)S(1)} async-done(((f32[128,8,128]{2,1,0:T(8,128)}), f32[128,8,128]{2,1,0:T(8,128)S(1)}, u32[]{:S(2)}, u32[]{:S(2)}) %all-to-all-start.1) | async-done | bytes 524320 | tf_op jit(solution)/shard_map/all_to_all | solution.py:374
  40.0 5.9 %all-to-all-start = ((f32[64,16,128]{2,1,0:T(8,128)}), f32[64,16,128]{2,1,0:T(8,128)S(1)}, u32[]{:S(2)}, u32[]{:S(2)}) async-start(f32[64,16,128]{2,1,0:T(8,128)} %pad_maximum_fusion), calls=%async_computation | async-start | bytes 1048576 | tf_op jit(solution)/shard_map/all_to_all | solution.py:335
  46.5 0.0 copy-done.1
  46.5 0.0 copy-done.2
  46.5 0.0 copy-done.3
  46.5 0.0 copy-done.4
  46.6 0.0 copy-start
  46.6 11.9 %shard_map.84.part_ref = f32[256,128]{1,0:T(8,128)S(1)} custom-call(s32[1]{0:T(128)} %bitcast.3.rep_ref, bf16[32,128,256]{2,1,0:T(8,128)(2,1)} %get-tuple-element.18.w_in, f32[256,128]{1,0:T(8,128)S(1)} %get-tuple-element.13.mrow_ref, f32[1024,128]{1,0:T(8,128)S(1)} %bitcast.12, s32[32,256]{1,0:T(8,128)S(1)} %copy-done.2, s32[1,256]{1,0:T(1,128)S(1)} %bitcast.17, ...), custom_call_target="tpu_custom_call" | custom-call | flops 6442450944 | bytes 1874048 | tf_op jit(solution)/shard_map/pallas_call | solution.py:321
  58.5 6.8 %all-to-all-done = f32[64,16,128]{2,1,0:T(8,128)S(1)} async-done(((f32[64,16,128]{2,1,0:T(8,128)}), f32[64,16,128]{2,1,0:T(8,128)S(1)}, u32[]{:S(2)}, u32[]{:S(2)}) %all-to-all-start) | async-done | bytes 524320 | tf_op jit(solution)/shard_map/all_to_all | solution.py:335
  65.3 0.0 copy-done
  65.4 0.3 shard_map.85
  65.7 10.1 %all_to_all.15 = f32[4,64,128]{2,1,0:T(8,128)S(1)} all-to-all(f32[4,64,128]{2,1,0:T(8,128)S(1)} %bitcast.13), channel_id=1, replica_groups=mesh['box'=128,'rep'=4] {'rep'}, dimensions={0} | all-to-all | bytes 262144 | tf_op jit(solution)/shard_map/all_to_all | solution.py:418
  75.8 0.6 slice_bitcast_fusion
  (1 shorter events, 0.0 us)
Async XLA Ops:
  2.3 37.7 %all-to-all-start.1 = ((f32[128,8,128]{2,1,0:T(8,128)}), f32[128,8,128]{2,1,0:T(8,128)S(1)}, u32[]{:S(2)}, u32[]{:S(2)}) async-start(f32[128,8,128]{2,1,0:T(8,128)} %bitcast.4), calls=%async_computation.1 | async-start | bytes 1048576 | tf_op jit(solution)/shard_map/all_to_all | solution.py:374
  29.0 17.5 %copy-start.1 = (f32[8,14641]{1,0:T(8,128)S(1)}, f32[8,14641]{1,0:T(8,128)}, u32[]{:S(2)}) copy-start(f32[8,14641]{1,0:T(8,128)} %sh_ref.1) | copy-start | bytes 1405540
  29.0 17.5 %copy-start.2 = (s32[32,256]{1,0:T(8,128)S(1)}, s32[32,256]{1,0:T(8,128)}, u32[]{:S(2)}) copy-start(s32[32,256]{1,0:T(8,128)} %ps_ref.1) | copy-start | bytes 98308
  29.0 17.5 %copy-start.3 = (f32[121,16]{0,1:T(8,128)S(1)}, f32[121,16]{0,1:T(8,128)}, u32[]{:S(2)}) copy-start(f32[121,16]{0,1:T(8,128)} %param.9) | copy-start | bytes 23236
  29.0 17.5 %copy-start.4 = (s32[256]{0:T(256)S(1)}, s32[256]{0:T(256)}, u32[]{:S(2)}) copy-start(s32[256]{0:T(256)} %param.11) | copy-start | bytes 3076
  29.0 3.6 %collective-permute-start = (f32[64,8,128]{2,1,0:T(8,128)S(1)}, f32[64,8,128]{2,1,0:T(8,128)S(1)}, u32[]{:S(2)}, u32[]{:S(2)}) collective-permute-start(f32[64,8,128]{2,1,0:T(8,128)S(1)} %get-tuple-element.15), channel_id=1, source_target_pairs={{0,4},{4,0},{8,12},{12,8},{16,20},{20,16},{24,28},{28,24},{32,36},... | collective-permute-start | bytes 786440 | tf_op jit(solution)/shard_map/ppermute | solution.py:332
  40.0 25.4 %all-to-all-start = ((f32[64,16,128]{2,1,0:T(8,128)}), f32[64,16,128]{2,1,0:T(8,128)S(1)}, u32[]{:S(2)}, u32[]{:S(2)}) async-start(f32[64,16,128]{2,1,0:T(8,128)} %pad_maximum_fusion), calls=%async_computation | async-start | bytes 1048576 | tf_op jit(solution)/shard_map/all_to_all | solution.py:335
  46.6 18.8 %copy-start = (s32[128,8]{0,1:T(8,128)S(1)}, s32[128,8]{0,1:T(8,128)}, u32[]{:S(2)}) copy-start(s32[128,8]{0,1:T(8,128)} %param.13) | copy-start | bytes 12292

commit v4 on v3

--- a/solution.py
+++ b/solution.py
@@ -154,7 +154,7 @@
 
     sign = parity_lanes(slots)
     moments = split_hl(mrow_ref[...] * sign)
-    acc_ref[...] = jnp.zeros_like(acc_ref)
+    groups = classes // step
     row_id = lax.broadcasted_iota(jnp.int32, (block, slots), 0).astype(F32).astype(BF)
 
     def prepare(g, out):
@@ -175,9 +175,21 @@
                 [pick16(row_id == spread_rows(here[i : i + 1, :], block)) for i in range(step)],
                 axis=1,
             )
-            acc_ref[start : start + block, :] += mm(hot, m)
-
-    groups = classes // step
+            total = mm(hot, m)
+            if g > 0:
+                total = acc_ref[start : start + block, :] + total
+            if g + 1 < groups:
+                acc_ref[start : start + block, :] = total
+                continue
+            sums = fold(total) * sign
+            if start == 0:
+                own_ref[...] = sums
+            else:
+                pairs = sums.reshape(block // (2 * SEND), 2 * SEND, LANES)
+                chips = slice((start - slots) // (2 * SEND), (start - slots + block) // (2 * SEND))
+                keep_ref[chips, :, :] = pairs[:, :SEND, :]
+                give_ref[chips, :, :] = pairs[:, SEND:, :]
+
     held = (m_even, m_odd)
     fetch(0).wait()
     prepare(0, held[0])
@@ -190,12 +202,6 @@
             prepare(g + 1, held[(g + 1) % 2])
         scatter(g, held[g % 2])
 
-    own_ref[...] = fold(acc_ref[:slots, :]) * sign
-    far = columns - slots
-    sums = fold(acc_ref[slots:, :]) * parity_lanes(far)
-    pairs = sums.reshape(far // (2 * SEND), 2 * SEND, LANES)
-    keep_ref[...] = pairs[:, :SEND, :]
-    give_ref[...] = pairs[:, SEND:, :]
     for g in range(classes // step):
         keep_w(g).wait()
 

time: 76.8 us -> 76.8 us (level)
  no operation moved by 1% of the time
where the time goes in v4:
time: 76.8 us; the launch traced here: 76.4 us
  starting transfers between devices  25.4 us (33%)
  Pallas kernels  23.8 us (31%)
  waiting for transfers between devices  14.8 us (19%)
  blocking collectives  10.1 us (13%)
  other arithmetic  0.85 us (1%)
  between operations  0.79 us (1%)
    pallas_call x4, Pallas kernels, run(): return made(*placed)  23.8 us
    all_to_all x1, starting transfers between devices, on_device(): lax.all_to_all(outgoing.reshape(nb, SEND, LANES), 'box', split_axis=0, co...  17.4 us
    all_to_all x1, blocking collectives, on_device(): lax.all_to_all(summed.reshape(quarters, quarter, LANES), 'rep', split_axi...  10.1 us
    all_to_all x1, waiting for transfers between devices, across_chips(): lax.all_to_all(both, 'box', split_axis=0, concat_axis=0, axis_index_group...  6.84 us
    all_to_all x1, waiting for transfers between devices, on_device(): lax.all_to_all(outgoing.reshape(nb, SEND, LANES), 'box', split_axis=0, co...  6.56 us
    all_to_all x1, starting transfers between devices, across_chips(): lax.all_to_all(both, 'box', split_axis=0, concat_axis=0, axis_index_group...  5.87 us
    ppermute x1, starting transfers between devices, across_chips(): got = lax.ppermute(give, 'box', [(i, i ^ 1) for i in range(nb)])  2.19 us
  transfers between devices with their start and end apart: 3, of which 3 were waited for; matrix products, arithmetic and copies ran while one was open for 1% of the time, Pallas kernels for 28%

profile of v4, /device:TPU:8, one launch (start us, length us, event | category | flops | bytes accessed | tf_op | source)
XLA Modules:
  0.0 76.4 jit_solution(9329194206525976261)
XLA Ops:
  0.0 2.3 %shard_map.82 = (f32[1024,128]{1,0:T(8,128)}, f32[256,128]{1,0:T(8,128)S(1)}) custom-call(f32[121,256]{1,0:T(8,128)} %mult_in.1, s32[8,128]{1,0:T(8,128)} %bitcast.14), custom_call_target="tpu_custom_call" | custom-call | flops 100000000 | bytes 1000000 | tf_op jit(solution)/shard_map/pallas_call | solution.py:327
  2.3 17.4 %all-to-all-start.1 = ((f32[128,8,128]{2,1,0:T(8,128)}), f32[128,8,128]{2,1,0:T(8,128)S(1)}, u32[]{:S(2)}, u32[]{:S(2)}) async-start(f32[128,8,128]{2,1,0:T(8,128)} %bitcast.4), calls=%async_computation.1 | async-start | bytes 1048576 | tf_op jit(solution)/shard_map/all_to_all | solution.py:380
  19.7 9.3 %shard_map.83 = (bf16[32,128,256]{2,1,0:T(8,128)(2,1)}, f32[256,128]{1,0:T(8,128)S(1)}, f32[64,8,128]{2,1,0:T(8,128)S(1)}, f32[64,8,128]{2,1,0:T(8,128)S(1)}) custom-call(s32[1]{0:T(128)} %bitcast.group_ref, f32[32,14641]{1,0:T(8,128)} %op_in.1, f32[256,128]{1,0:T(8,128)S(1)} %get-tuple-element.13.mrow_ref, s32[32,256]{1,0:T(8,128)} %ps_ref.1), custom_call_target="tpu_custom_call" | custom-call | flops 6442450944 | bytes 1874048 | tf_op jit(solution)/shard_map/pallas_call | solution.py:327
  29.0 0.0 copy-start.1
  29.0 0.0 copy-start.2
  29.0 0.0 copy-start.3
  29.0 0.0 copy-start.4
  29.0 2.2 %collective-permute-start = (f32[64,8,128]{2,1,0:T(8,128)S(1)}, f32[64,8,128]{2,1,0:T(8,128)S(1)}, u32[]{:S(2)}, u32[]{:S(2)}) collective-permute-start(f32[64,8,128]{2,1,0:T(8,128)S(1)} %get-tuple-element.15), channel_id=1, source_target_pairs={{0,4},{4,0},{8,12},{12,8},{16,20},{20,16},{24,28},{28,24},{32,36},... | collective-permute-start | bytes 786440 | tf_op jit(solution)/shard_map/ppermute | solution.py:338
  31.2 1.4 %collective-permute-done = f32[64,8,128]{2,1,0:T(8,128)S(1)} collective-permute-done((f32[64,8,128]{2,1,0:T(8,128)S(1)}, f32[64,8,128]{2,1,0:T(8,128)S(1)}, u32[]{:S(2)}, u32[]{:S(2)}) %collective-permute-start) | collective-permute-done | bytes 262176 | tf_op jit(solution)/shard_map/ppermute | solution.py:338
  32.6 0.8 %pad_maximum_fusion = f32[64,16,128]{2,1,0:T(8,128)} fusion(f32[64,8,128]{2,1,0:T(8,128)S(1)} %collective-permute-done, f32[64,8,128]{2,1,0:T(8,128)S(1)} %get-tuple-element.14), kind=kLoop, calls=%fused_computation | loop fusion | flops 131072 | bytes 1048576 | tf_op jit(solution)/shard_map/concatenate | solution.py:339
  33.4 6.6 %all-to-all-done.1 = f32[128,8,128]{2,1,0:T(8,128)S(1)} async-done(((f32[128,8,128]{2,1,0:T(8,128)}), f32[128,8,128]{2,1,0:T(8,128)S(1)}, u32[]{:S(2)}, u32[]{:S(2)}) %all-to-all-start.1) | async-done | bytes 524320 | tf_op jit(solution)/shard_map/all_to_all | solution.py:380
  40.0 5.9 %all-to-all-start = ((f32[64,16,128]{2,1,0:T(8,128)}), f32[64,16,128]{2,1,0:T(8,128)S(1)}, u32[]{:S(2)}, u32[]{:S(2)}) async-start(f32[64,16,128]{2,1,0:T(8,128)} %pad_maximum_fusion), calls=%async_computation | async-start | bytes 1048576 | tf_op jit(solution)/shard_map/all_to_all | solution.py:341
  46.5 0.0 copy-done.1
  46.5 0.0 copy-done.2
  46.5 0.0 copy-done.3
  46.5 0.0 copy-done.4
  46.6 0.0 copy-start
  46.6 11.9 %shard_map.84.part_ref = f32[256,128]{1,0:T(8,128)S(1)} custom-call(s32[1]{0:T(128)} %bitcast.3.rep_ref, bf16[32,128,256]{2,1,0:T(8,128)(2,1)} %get-tuple-element.18.w_in, f32[256,128]{1,0:T(8,128)S(1)} %get-tuple-element.13.mrow_ref, f32[1024,128]{1,0:T(8,128)S(1)} %bitcast.12, s32[32,256]{1,0:T(8,128)S(1)} %copy-done.2, s32[1,256]{1,0:T(1,128)S(1)} %bitcast.17, ...), custom_call_target="tpu_custom_call" | custom-call | flops 6442450944 | bytes 1874048 | tf_op jit(solution)/shard_map/pallas_call | solution.py:327
  58.5 6.8 %all-to-all-done = f32[64,16,128]{2,1,0:T(8,128)S(1)} async-done(((f32[64,16,128]{2,1,0:T(8,128)}), f32[64,16,128]{2,1,0:T(8,128)S(1)}, u32[]{:S(2)}, u32[]{:S(2)}) %all-to-all-start) | async-done | bytes 524320 | tf_op jit(solution)/shard_map/all_to_all | solution.py:341
  65.3 0.0 copy-done
  65.4 0.3 shard_map.85
  65.7 10.1 %all_to_all.15 = f32[4,64,128]{2,1,0:T(8,128)S(1)} all-to-all(f32[4,64,128]{2,1,0:T(8,128)S(1)} %bitcast.13), channel_id=1, replica_groups=mesh['box'=128,'rep'=4] {'rep'}, dimensions={0} | all-to-all | bytes 262144 | tf_op jit(solution)/shard_map/all_to_all | solution.py:424
  75.8 0.6 slice_bitcast_fusion
  (1 shorter events, 0.0 us)
Async XLA Ops:
  2.3 37.7 %all-to-all-start.1 = ((f32[128,8,128]{2,1,0:T(8,128)}), f32[128,8,128]{2,1,0:T(8,128)S(1)}, u32[]{:S(2)}, u32[]{:S(2)}) async-start(f32[128,8,128]{2,1,0:T(8,128)} %bitcast.4), calls=%async_computation.1 | async-start | bytes 1048576 | tf_op jit(solution)/shard_map/all_to_all | solution.py:380
  29.0 17.5 %copy-start.1 = (f32[8,14641]{1,0:T(8,128)S(1)}, f32[8,14641]{1,0:T(8,128)}, u32[]{:S(2)}) copy-start(f32[8,14641]{1,0:T(8,128)} %sh_ref.1) | copy-start | bytes 1405540
  29.0 17.5 %copy-start.2 = (s32[32,256]{1,0:T(8,128)S(1)}, s32[32,256]{1,0:T(8,128)}, u32[]{:S(2)}) copy-start(s32[32,256]{1,0:T(8,128)} %ps_ref.1) | copy-start | bytes 98308
  29.0 17.5 %copy-start.3 = (f32[121,16]{0,1:T(8,128)S(1)}, f32[121,16]{0,1:T(8,128)}, u32[]{:S(2)}) copy-start(f32[121,16]{0,1:T(8,128)} %param.9) | copy-start | bytes 23236
  29.0 17.5 %copy-start.4 = (s32[256]{0:T(256)S(1)}, s32[256]{0:T(256)}, u32[]{:S(2)}) copy-start(s32[256]{0:T(256)} %param.11) | copy-start | bytes 3076
  29.0 3.6 %collective-permute-start = (f32[64,8,128]{2,1,0:T(8,128)S(1)}, f32[64,8,128]{2,1,0:T(8,128)S(1)}, u32[]{:S(2)}, u32[]{:S(2)}) collective-permute-start(f32[64,8,128]{2,1,0:T(8,128)S(1)} %get-tuple-element.15), channel_id=1, source_target_pairs={{0,4},{4,0},{8,12},{12,8},{16,20},{20,16},{24,28},{28,24},{32,36},... | collective-permute-start | bytes 786440 | tf_op jit(solution)/shard_map/ppermute | solution.py:338
  40.0 25.4 %all-to-all-start = ((f32[64,16,128]{2,1,0:T(8,128)}), f32[64,16,128]{2,1,0:T(8,128)S(1)}, u32[]{:S(2)}, u32[]{:S(2)}) async-start(f32[64,16,128]{2,1,0:T(8,128)} %pad_maximum_fusion), calls=%async_computation | async-start | bytes 1048576 | tf_op jit(solution)/shard_map/all_to_all | solution.py:341
  46.6 18.8 %copy-start = (s32[128,8]{0,1:T(8,128)S(1)}, s32[128,8]{0,1:T(8,128)}, u32[]{:S(2)}) copy-start(s32[128,8]{0,1:T(8,128)} %param.13) | copy-start | bytes 12292
